TPU v7x, 256 devices: a whole 4x4x8 slice. The times are simulated.
256 devices in a mesh: dp: 32 (over z, y_hi, core), expert: 8 (over y_lo, x).
Axes of the slice: x: 4, y: 4 (y_hi: 2, y_lo: 2; y = y_hi * 2 + y_lo), z: 8, core: 2. Of those that a mesh axis runs over, the one named last changes fastest.
Arguments:
- tokens: bfloat16 [1024, 3072], P('expert'), may hold values from -6 to 6
- expert_ids: int32 [1024, 2], P('expert'), may hold values from 0 to 7, all different within a row; in each aligned block of 128 rows (0 to 127, 128 to 255, ...) at most 40 rows name the same one
- combine: float32 [1024, 2], P('expert'), may hold values from 0.1 to 1
- cotangent: bfloat16 [1024, 3072], P('expert'), may hold values from -6 to 6
- w_gate: bfloat16 [8, 3072, 8192], P('expert', None, 'dp'), may hold values from -0.109375 to 0.109375
- w_up: bfloat16 [8, 3072, 8192], P('expert', None, 'dp'), may hold values from -0.109375 to 0.109375
- w_down: bfloat16 [8, 8192, 3072], P('expert', 'dp'), may hold values from -0.0625 to 0.0625
Outputs:
- mixed: bfloat16 [1024, 3072], P('expert', 'dp')
- grad_tokens: bfloat16 [1024, 3072], P('expert', 'dp')
- grad_combine: float32 [1024, 2], P('expert')
- grad_gate: bfloat16 [8, 3072, 8192], P('expert', None, 'dp')
- grad_up: bfloat16 [8, 3072, 8192], P('expert', None, 'dp')
- grad_down: bfloat16 [8, 8192, 3072], P('expert', 'dp')
Inputs may be any that keep to these rules, and one draw needn't show every extreme that they name: `expert_ids`: A row names two different experts. Among the rows of one index of expert, each expert is named at most 40 times, a bound that some block reaches.
All inputs are finite; a program needn't handle non-finite values.
Results may differ from a plain program's by a relative error of at most 0.0058.
Values may be sent and summed in bfloat16 or wider, within the bound.
A program may use at most 128 MiB of HBM per device.

v0:
```python
import jax
import jax.numpy as jnp
from jax import lax
from jax.sharding import PartitionSpec as P


def contract_rows(left, right):
    return lax.dot_general(
        left, right, (((0,), (0,)), ((), ())), preferred_element_type=jnp.float32
    )


def contract_cols(left, right):
    return lax.dot_general(
        left, right, (((1,), (1,)), ((), ())), preferred_element_type=jnp.float32
    )


def local(tokens, expert_ids, combine, cotangent, w_gate, w_up, w_down):
    experts = lax.axis_size("expert")
    replicas = lax.axis_size("dp")
    tok_count = tokens.shape[0]
    features = tokens.shape[1]
    share_width = features // replicas
    capacity = min(tok_count, 5 * tok_count // (2 * experts))
    slot_total = experts * capacity
    flat_ids = expert_ids.reshape(-1)
    onehot = (flat_ids[:, None] == jnp.arange(experts, dtype=jnp.int32)[None, :]).astype(jnp.int32)
    rank_in = jnp.sum((jnp.cumsum(onehot, axis=0) - 1) * onehot, axis=1)
    slot_index = flat_ids * capacity + rank_in
    source_row = (
        jnp.full((slot_total,), -1, jnp.int32)
        .at[slot_index]
        .set(jnp.arange(2 * tok_count, dtype=jnp.int32))
    )
    is_live = (source_row >= 0)[:, None]
    source_safe = jnp.maximum(source_row, 0)
    token_of = source_safe // 2
    x_buffer = jnp.where(is_live, tokens[token_of], jnp.zeros((), jnp.bfloat16))
    scaled_rows = (
        cotangent[token_of].astype(jnp.float32) * combine.reshape(-1)[source_safe][:, None]
    )
    e_buffer = jnp.where(is_live, scaled_rows, 0.0).astype(jnp.bfloat16)
    rows_x, rows_e = (
        lax.all_to_all(x_buffer, "expert", split_axis=0, concat_axis=0, tiled=True),
        lax.all_to_all(e_buffer, "expert", split_axis=0, concat_axis=0, tiled=True),
    )
    gate_w = w_gate[0]
    up_w = w_up[0]
    down_w = w_down[0]
    gate_proj = jnp.dot(rows_x, gate_w, preferred_element_type=jnp.float32)
    up_proj = jnp.dot(rows_x, up_w, preferred_element_type=jnp.float32)
    sigmoid_g = jax.nn.sigmoid(gate_proj)
    active = gate_proj * sigmoid_g
    hidden = (active * up_proj).astype(jnp.bfloat16)
    out_part = jnp.dot(hidden, down_w, preferred_element_type=jnp.float32)
    hidden_grad = contract_cols(rows_e, down_w)
    gate_grad = (hidden_grad * up_proj * sigmoid_g * (1.0 + gate_proj * (1.0 - sigmoid_g))).astype(
        jnp.bfloat16
    )
    up_grad = (hidden_grad * active).astype(jnp.bfloat16)
    grad_down = contract_rows(hidden, rows_e).astype(jnp.bfloat16)[None]
    grad_gate = contract_rows(rows_x, gate_grad).astype(jnp.bfloat16)[None]
    grad_up = contract_rows(rows_x, up_grad).astype(jnp.bfloat16)[None]
    input_part = contract_cols(gate_grad, gate_w) + contract_cols(up_grad, up_w)
    stacked = jnp.stack([out_part, input_part], axis=1)
    shares = lax.psum_scatter(stacked, "dp", scatter_dimension=2, tiled=True)
    returned = lax.all_to_all(shares, "expert", split_axis=0, concat_axis=0, tiled=True)
    picked = returned[slot_index].reshape(tok_count, 2, 2, share_width)
    outputs = picked[:, :, 0]
    token_grad = picked[:, 0, 1] + picked[:, 1, 1]
    mixed = jnp.sum(combine[:, :, None] * outputs, axis=1).astype(jnp.bfloat16)
    cot_share = lax.dynamic_slice_in_dim(
        cotangent, lax.axis_index("dp") * share_width, share_width, 1
    ).astype(jnp.float32)
    dot_terms = jnp.sum(cot_share[:, None, :] * outputs, axis=2)
    grad_combine = lax.psum(dot_terms, "dp")
    return (mixed, token_grad.astype(jnp.bfloat16), grad_combine, grad_gate, grad_up, grad_down)


def solution(mesh):
    in_specs = (
        P("expert", None),
        P("expert", None),
        P("expert", None),
        P("expert", None),
        P("expert", None, "dp"),
        P("expert", None, "dp"),
        P("expert", "dp", None),
    )
    out_specs = (
        P("expert", "dp"),
        P("expert", "dp"),
        P("expert", None),
        P("expert", None, "dp"),
        P("expert", None, "dp"),
        P("expert", "dp", None),
    )
    return jax.shard_map(local, mesh=mesh, in_specs=in_specs, out_specs=out_specs, check_vma=False)
```

profile of v0, /device:TPU:1, one launch (start us, length us, event | category | flops | bytes accessed | tf_op | source)
XLA Modules:
  0.0 560.8 jit_solution(12085554549701467663)
XLA Ops:
  7.2 0.9 copy.26
  8.4 0.7 broadcast_multiply_fusion
  10.3 1.4 scatter_custom_fusion
  11.7 0.8 copy.24
  12.7 2.5 gather_fusion.2
  15.3 3.4 gather_fusion.1
  18.7 3.6 fusion.2
  22.3 6.0 %all-to-all-start.1 = ((bf16[8,40,3072]{2,1,0:T(8,128)(2,1)}), bf16[8,40,3072]{2,1,0:T(8,128)(2,1)}, u32[]{:S(2)}, u32[]{:S(2)}) async-start(bf16[8,40,3072]{2,1,0:T(8,128)(2,1)} %fusion.2), calls=%async_computation.1 | async-start | bytes 3932160 | tf_op jit(solution)/shard_map/all_to_all | solution.py:46
  28.3 3.5 gather_fusion
  31.7 3.0 broadcast_select_fusion
  34.8 19.2 %all-to-all-done.1 = bf16[8,40,3072]{2,1,0:T(8,128)(2,1)} async-done(((bf16[8,40,3072]{2,1,0:T(8,128)(2,1)}), bf16[8,40,3072]{2,1,0:T(8,128)(2,1)}, u32[]{:S(2)}, u32[]{:S(2)}) %all-to-all-start.1) | async-done | bytes 1966112 | tf_op jit(solution)/shard_map/all_to_all | solution.py:46
  54.0 4.3 all-to-all-start
  58.6 2.7 fusion.6
  61.3 22.7 %all-to-all-done = bf16[8,40,3072]{2,1,0:T(8,128)(2,1)} async-done(((bf16[8,40,3072]{2,1,0:T(8,128)(2,1)}), bf16[8,40,3072]{2,1,0:T(8,128)(2,1)}, u32[]{:S(2)}, u32[]{:S(2)}) %all-to-all-start) | async-done | bytes 1966112 | tf_op jit(solution)/shard_map/all_to_all | solution.py:45
  84.0 2.7 fusion.14
  86.7 2.4 multiply_convert_fusion.2
  89.1 0.7 fusion.12
  89.8 0.7 copy-done.3
  91.2 0.7 fusion
  92.0 3.6 pad_maximum_fusion
  95.6 14.2 %copy.29 = f32[320,2,3072]{0,1,2:T(2,128)} copy(f32[320,2,3072]{2,0,1:T(8,128)} %pad_maximum_fusion) | data formatting | bytes 15728640 | tf_op jit(solution)/shard_map/stack | solution.py:66
  111.8 3.7 fusion.3
  115.5 3.7 fusion.4
  119.2 290.2 %all-reduce.3.cloned.1.call-done = f32[320,2,3072]{0,1,2:T(2,128)} async-done(((f32[320,2,3072]{0,1,2:T(2,128)}), f32[320,2,3072]{0,1,2:T(2,128)}) %all-reduce.3.cloned.1.call-update) | async-done | bytes 7864336
  409.4 1.0 constant_dynamic-slice_fusion
  410.4 0.9 copy.30
  411.3 4.3 all-to-all-start.2
  415.6 3.7 fusion.5
  419.3 4.4 all-to-all-done.2
  423.7 1.0 gather_fusion.3
  425.6 126.5 %psum.7 = f32[128,2]{1,0:T(8,128)S(1)} all-reduce(f32[128,2]{1,0:T(8,128)S(1)} %get-tuple-element.12), channel_id=1, replica_groups=mesh['dp'=32,'expert'=8] {'dp'}, use_global_device_ids=true, to_apply=%region_7.8 | all-reduce | flops 256 | bytes 2048 | tf_op jit(solution)/shard_map/psum | solution.py:77
  552.7 0.7 copy.34
  (42 shorter events, 6.1 us)
Async XLA Ops:
  7.2 79.5 %copy-start = (bf16[1,3072,256]{2,1,0:T(8,128)(2,1)S(1)}, bf16[1,3072,256]{2,1,0:T(8,128)(2,1)}, u32[]{:S(2)}) copy-start(bf16[1,3072,256]{2,1,0:T(8,128)(2,1)} %param.12) | copy-start | bytes 4718596
  7.2 8.1 %copy-start.1 = (bf16[128,3072]{1,0:T(8,128)(2,1)S(1)}, bf16[128,3072]{1,0:T(8,128)(2,1)}, u32[]{:S(2)}) copy-start(bf16[128,3072]{1,0:T(8,128)(2,1)} %param.10) | copy-start | bytes 2359300
  22.3 6.0 %copy-start.2 = (bf16[128,3072]{1,0:T(8,128)(2,1)S(1)}, bf16[128,3072]{1,0:T(8,128)(2,1)}, u32[]{:S(2)}) copy-start(bf16[128,3072]{1,0:T(8,128)(2,1)} %param.7) | copy-start | bytes 2359300
  22.3 31.7 %all-to-all-start.1 = ((bf16[8,40,3072]{2,1,0:T(8,128)(2,1)}), bf16[8,40,3072]{2,1,0:T(8,128)(2,1)}, u32[]{:S(2)}, u32[]{:S(2)}) async-start(bf16[8,40,3072]{2,1,0:T(8,128)(2,1)} %fusion.2), calls=%async_computation.1 | async-start | bytes 3932160 | tf_op jit(solution)/shard_map/all_to_all | solution.py:46
  54.0 30.0 %all-to-all-start = ((bf16[8,40,3072]{2,1,0:T(8,128)(2,1)}), bf16[8,40,3072]{2,1,0:T(8,128)(2,1)}, u32[]{:S(2)}, u32[]{:S(2)}) async-start(bf16[8,40,3072]{2,1,0:T(8,128)(2,1)} %broadcast_select_fusion), calls=%async_computation | async-start | bytes 3932160 | tf_op jit(solution)/shard_map/all_to_all | solution.py:45
  58.4 351.0 %all-reduce.3.cloned.1.call-start = ((), (), s32[]{:S(2)}) async-start(), calls=%async_computation.3 | async-start | bytes 18874368
  86.7 2.4 copy-start.4
  89.1 1.4 copy-start.3
  109.8 0.7 copy-start.5
  411.3 12.4 %all-to-all-start.2 = ((f32[320,2,96]{2,1,0:T(2,128)}), f32[320,2,96]{2,1,0:T(2,128)S(1)}, u32[]{:S(2)}, u32[]{:S(2)}) async-start(f32[320,2,96]{2,1,0:T(2,128)} %copy.30), calls=%async_computation.2 | async-start | bytes 655360 | tf_op jit(solution)/shard_map/all_to_all | solution.py:68
Sparse Core Ops, SparseCore 0:
  109.9 299.4 all-reduce.2
where the time goes:
time: 566 us; the launch traced here: 561 us
  waiting for transfers between devices  337 us (60%)
  blocking collectives  126 us (22%)
  local copies, waits for them, and re-layouts  34.3 us (6%)
  matrix products  21 us (4%)
  between operations  14.9 us (3%)
  starting transfers between devices  14.8 us (3%)
  other arithmetic  12.7 us (2%)
    unnamed x2, waiting for transfers between devices  290 us
    psum x1, blocking collectives, local(): grad_combine = lax.psum(dot_terms, 'dp')  126 us
    all_to_all x1, waiting for transfers between devices, local(): lax.all_to_all(x_buffer, 'expert', split_axis=0, concat_axis=0, tiled=True)  22.7 us
    all_to_all x1, waiting for transfers between devices, local(): lax.all_to_all(e_buffer, 'expert', split_axis=0, concat_axis=0, tiled=True)  19.2 us
    another operation x1, local copies, waits for them, and re-layouts, local(): stacked = jnp.stack([out_part, input_part], axis=1)  14.2 us
  transfers between devices with their start and end apart: 4, of which 4 were waited for; matrix products, arithmetic and copies ran while one was open for 4% of the time, Pallas kernels for 0%

commit v1 on v0

v1 whole, which is shorter than its diff:
```python
import jax
import jax.numpy as jnp
from jax import lax
from jax.experimental import pallas as pl
from jax.experimental.pallas import tpu as pltpu
from jax.sharding import PartitionSpec as P

MESH = pl.DeviceIdType.MESH
F32 = jnp.float32
BF16 = jnp.bfloat16

T = 128
D = 3072
HD = 1536
CAP = 40
BLK = 2 * CAP
SLAB = 48
NE = 8
NZ = 8
W = 256
CH = 384
NP = 4

PLANE = ((2, 1), (1, 1), (3, 1), (2, 0), (0, 1), (1, 0), (3, 0))


def nn(a, b):
    return lax.dot_general(a, b, (((1,), (0,)), ((), ())), preferred_element_type=F32)


def nt(a, b):
    return lax.dot_general(a, b, (((1,), (1,)), ((), ())), preferred_element_type=F32)


def tn(a, b):
    return lax.dot_general(a, b, (((0,), (0,)), ((), ())), preferred_element_type=F32)


def iota(shape, axis):
    return lax.broadcasted_iota(jnp.int32, shape, axis)


def split3(a):
    hi = a.astype(BF16)
    rest = a - hi.astype(F32)
    mid = rest.astype(BF16)
    low = (rest - mid.astype(F32)).astype(BF16)
    return hi, mid, low


def kernel(
    tok_hbm, ids_ref, comb_ref, cot_hbm, wg_hbm, wu_hbm, wd_hbm,
    mixed_ref, gtok_ref, gcomb_ref, gg_hbm, gu_hbm, gd_hbm,
    tc, wg, wu, wd, wgx, wux, wdx, slt, cwt, sendb, rows, acts, actx,
    gsend, grecv, tmat, rsend, rrecv, zsend, zrecv, gzrecv, ysend, yrecv, gycs,
    fsend, frecv, og, ou, od,
    lsem, osem, ws_s, ws_r, d_s, d_r, c_s, c_r, x_s, x_r, g_s, g_r, r_s, r_r,
    z_s, z_r, gz_s, gz_r, p_s, p_r,
):
    d = lax.axis_index("dp")
    e = lax.axis_index("expert")
    z, h, c = d // 4, (d // 2) % 2, d % 2
    yl, x = e // 4, e % 4
    twin = (z * 4 + h * 2 + (1 - c), e)
    over = (z * 4 + (1 - h) * 2 + c, e)

    def plane(step):
        return ((yl + step[1]) % 2) * 4 + (x + step[0]) % 4

    def at_z(k):
        return (z + k) % NZ

    def zdev(zz):
        return (zz * 4 + h * 2 + c, e)

    def remote(src, dst, ssem, rsem, dev):
        return pltpu.make_async_remote_copy(
            src_ref=src, dst_ref=dst, send_sem=ssem, recv_sem=rsem, device_id=dev, device_id_type=MESH
        )

    half = pl.multiple_of(c * HD, HD)
    other_half = pl.multiple_of((1 - c) * HD, HD)

    loads = [
        pltpu.make_async_copy(tok_hbm.at[:, pl.ds(half, HD)], tc.at[pl.ds(0, T)], lsem.at[0]),
        pltpu.make_async_copy(cot_hbm.at[:, pl.ds(half, HD)], tc.at[pl.ds(T, T)], lsem.at[1]),
        pltpu.make_async_copy(wg_hbm, wg, lsem.at[2]),
        pltpu.make_async_copy(wu_hbm, wu, lsem.at[3]),
        pltpu.make_async_copy(wd_hbm, wd, lsem.at[4]),
    ]
    for cp in loads:
        cp.start()

    barrier = pltpu.get_barrier_semaphore()
    for step in PLANE:
        pl.semaphore_signal(barrier, inc=1, device_id=(d, plane(step)), device_id_type=MESH)
    for k in range(1, NZ):
        pl.semaphore_signal(barrier, inc=1, device_id=zdev(at_z(k)), device_id_type=MESH)
    pl.semaphore_signal(barrier, inc=1, device_id=twin, device_id_type=MESH)
    pl.semaphore_signal(barrier, inc=1, device_id=over, device_id_type=MESH)

    lane = iota((T, T), 1)
    ids = ids_ref[...]
    comb = comb_ref[...]
    pick0 = lane == ids[:, 0:1]
    pick1 = lane == ids[:, 1:2]
    chosen = jnp.logical_or(pick0, pick1)
    earlier = (iota((T, T), 0) > lane).astype(F32).astype(BF16)
    rank = nn(earlier, chosen.astype(F32).astype(BF16))
    slot = jnp.where(chosen, rank, -128.0)
    weight = jnp.where(pick0, comb[:, 0:1], 0.0) + jnp.where(pick1, comb[:, 1:2], 0.0)
    slot_t = slot.T
    weight_t = weight.T
    slt[...] = jnp.concatenate([slot_t[0:NE], slot_t[0:NE]], axis=1)
    cwt[...] = jnp.concatenate([jnp.ones((NE, T), F32), weight_t[0:NE]], axis=1)

    loads[0].wait()
    loads[1].wait()
    pl.semaphore_wait(barrier, len(PLANE) + NZ - 1 + 2)

    def pack(j):
        slots = slt[pl.ds(j, 1), :]
        weights = cwt[pl.ds(j, 1), :]
        row = iota((BLK, 2 * T), 0)
        col = iota((BLK, 2 * T), 1)
        want = jnp.where(col < T, row, row - CAP).astype(F32)
        hit = want == slots
        scale = jnp.sum(jnp.where(hit, weights, 0.0), axis=1, keepdims=True)
        block = nn(hit.astype(F32).astype(BF16), tc[...])
        sendb[j] = (block * scale).astype(BF16)

    sends = []
    for i, step in enumerate(PLANE):
        j = plane(step)
        pack(j)
        cp = remote(sendb.at[j], rows.at[c, e], d_s.at[i], d_r.at[e], (d, j))
        cp.start()
        sends.append(cp)
    pack(e)
    own = pltpu.make_async_copy(sendb.at[e], rows.at[c, e], lsem.at[5])
    own.start()
    cp = remote(sendb.at[e], rows.at[c, e], c_s.at[7], c_r.at[e], twin)
    cp.start()
    sends.append(cp)

    for m in range(NP):
        for n, (src, dst) in enumerate((
            (wd_hbm.at[:, pl.ds(pl.multiple_of((2 * m + 1 - c) * CH, CH), CH)], wdx.at[m]),
            (wg_hbm.at[pl.ds(pl.multiple_of((2 * m + c) * CH, CH), CH)], wgx.at[m]),
            (wu_hbm.at[pl.ds(pl.multiple_of((2 * m + c) * CH, CH), CH)], wux.at[m]),
        )):
            cp = remote(src, dst, ws_s.at[n, m], ws_r.at[n, m], twin)
            cp.start()
            sends.append(cp)

    expand = (iota((T, NE * BLK), 0) == iota((T, NE * BLK), 1) // BLK).astype(F32).astype(BF16)
    w_hi = weight.astype(BF16)
    w_lo = (weight - w_hi.astype(F32)).astype(BF16)
    inner = (iota((T, NE * BLK), 1) % BLK).astype(F32)
    slots_all = nn(slot.astype(BF16), expand)
    out_hit = slots_all == inner
    tmat[0:T] = jnp.where(out_hit, nn(w_hi, expand), 0.0).astype(BF16)
    tmat[T:2 * T] = jnp.where(out_hit, nn(w_lo, expand), 0.0).astype(BF16)
    tmat[2 * T:3 * T] = (slots_all == inner - CAP).astype(F32).astype(BF16)

    for i, step in enumerate(PLANE):
        j = plane((4 - step[0], step[1]))
        here = rows.at[c, j]
        remote(here, here, d_s.at[i], d_r.at[j], (d, j)).wait_recv()
        cp = remote(here, here, c_s.at[i], c_r.at[j], twin)
        cp.start()
        sends.append(cp)
    own.wait()
    for cp in loads[2:]:
        cp.wait()
    for i, step in enumerate(PLANE + ((0, 0),)):
        j = plane((4 - step[0], step[1]))
        there = rows.at[1 - c, j]
        remote(there, there, c_s.at[i], c_r.at[j], twin).wait_recv()

    def x_rows(k):
        return rows[k, :, 0:SLAB, :].reshape(NE * SLAB, HD)

    def e_rows(k):
        return rows[k, :, BLK - SLAB:BLK, :].reshape(NE * SLAB, HD)

    def first(a):
        return a.reshape(NE, SLAB, W)[:, 0:CAP].reshape(NE * CAP, W)

    def last(a):
        return a.reshape(NE, SLAB, W)[:, SLAB - CAP:].reshape(NE * CAP, W)

    gate = first(nn(x_rows(0), wg[0:HD]) + nn(x_rows(1), wg[HD:D]))
    up = first(nn(x_rows(0), wu[0:HD]) + nn(x_rows(1), wu[HD:D]))
    hgrad = last(nt(e_rows(0), wd[:, 0:HD]) + nt(e_rows(1), wd[:, HD:D]))
    sig = jax.nn.sigmoid(gate)
    active = gate * sig
    hidden = (active * up).astype(BF16)
    gate_grad = (hgrad * up * sig * (1.0 + gate * (1.0 - sig))).astype(BF16)
    up_grad = (hgrad * active).astype(BF16)
    acts[0] = hidden
    acts[1] = gate_grad
    acts[2] = up_grad
    xact = remote(acts, actx, x_s, x_r, twin)
    xact.start()
    hid32 = hidden.astype(F32)
    dots = jnp.sum(hid32 * hgrad, axis=1, keepdims=True)
    gsend[...] = jnp.broadcast_to(dots, (NE * CAP, T)).reshape(NE, CAP, T)
    for i, step in enumerate(PLANE):
        j = plane(step)
        cp = remote(gsend.at[j], grecv.at[e], g_s.at[i], g_r.at[e], (d, j))
        cp.start()
        sends.append(cp)
    grecv[e] = gsend[e]
    for n in range(3):
        for m in range(NP):
            cp = remote(
                (wdx, wgx, wux)[n].at[m], (wdx, wgx, wux)[n].at[m], ws_s.at[n, m], ws_r.at[n, m], twin
            )
            cp.wait_recv()
    xact.wait_recv()

    for s in range(NP):
        m = (z // 2 + s + 1) % NP
        oc = pl.multiple_of((2 * m + c) * CH, CH)
        tcol = pl.multiple_of((2 * m + 1 - c) * CH, CH)
        out = nn(acts[0], wd[:, pl.ds(oc, CH)]) + nn(actx[0], wdx[m])
        back = (
            nt(acts[1], wg[pl.ds(tcol, CH), :]) + nt(acts[2], wu[pl.ds(tcol, CH), :])
            + nt(actx[1], wgx[m]) + nt(actx[2], wux[m])
        )
        both = jnp.concatenate([out.reshape(NE, CAP, CH), back.reshape(NE, CAP, CH)], axis=1)
        rsend[s] = both.astype(BF16)
        for i, step in enumerate(PLANE):
            j = plane(step)
            cp = remote(rsend.at[s, j], rrecv.at[s, e], r_s.at[s, i], r_r.at[s, e], (d, j))
            cp.start()
            sends.append(cp)
        rrecv[s, e] = rsend[s, e]

    for step in PLANE:
        j = plane((4 - step[0], step[1]))
        remote(gsend.at[j], grecv.at[j], g_s.at[0], g_r.at[j], (d, j)).wait_recv()
    q = iota((T, NE * CAP), 1).astype(F32)
    place0 = jnp.sum(jnp.where(pick0, lane.astype(F32) * CAP + rank, 0.0), axis=1, keepdims=True)
    place1 = jnp.sum(jnp.where(pick1, lane.astype(F32) * CAP + rank, 0.0), axis=1, keepdims=True)
    hits = jnp.concatenate([(q == place0), (q == place1)], axis=0).astype(F32).astype(BF16)
    parts = split3(grecv[...].reshape(NE * CAP, T))
    got = nn(hits, parts[0]) + nn(hits, parts[1]) + nn(hits, parts[2])
    col0 = got[0:T] / comb[:, 0:1]
    col1 = got[T:2 * T] / comb[:, 1:2]
    two = jnp.where(lane == 0, col0, jnp.where(lane == 1, col1, 0.0))
    gzrecv[z] = two.T[0:8]
    for k in range(1, NZ):
        cp = remote(gzrecv.at[z], gzrecv.at[z], gz_s.at[k], gz_r.at[z], zdev(at_z(k)))
        cp.start()
        sends.append(cp)

    def padded(a, lead):
        a = a.astype(F32).reshape(NE, CAP, W)
        zero = jnp.zeros((NE, SLAB - CAP, W), F32)
        a = jnp.concatenate([a, zero] if lead else [zero, a], axis=1)
        return a.reshape(NE * SLAB, W).astype(BF16)

    hid_pad = padded(acts[0], False)
    pair_pad = jnp.concatenate([padded(acts[1], True), padded(acts[2], True)], axis=1)
    stores = []
    for k in range(2):
        both = tn(x_rows(k), pair_pad)
        og[k * HD:(k + 1) * HD] = both[:, 0:W].astype(BF16)
        ou[k * HD:(k + 1) * HD] = both[:, W:2 * W].astype(BF16)
        od[:, k * HD:(k + 1) * HD] = tn(hid_pad, e_rows(k)).astype(BF16)
    for n, (src, dst) in enumerate(((og, gg_hbm), (ou, gu_hbm), (od, gd_hbm))):
        cp = pltpu.make_async_copy(src, dst, osem.at[n])
        cp.start()
        stores.append(cp)

    mine = z % 2 == c
    for s in range(NP):
        for step in PLANE:
            j = plane((4 - step[0], step[1]))
            remote(rsend.at[s, j], rrecv.at[s, j], r_s.at[s, 0], r_r.at[s, j], (d, j)).wait_recv()
        m = (z // 2 + s + 1) % NP
        sums = nn(tmat[...], rrecv[s].reshape(NE * BLK, CH))
        mix = sums[0:T] + sums[T:2 * T]
        back = sums[2 * T:3 * T]
        if s < NP - 1:
            zsend[s, 0] = mix.astype(BF16)
            zsend[s, 1] = back.astype(BF16)
            for n in range(2):
                to = 2 * m + (c if n == 0 else 1 - c)
                cp = remote(zsend.at[s, n], zrecv.at[z], z_s.at[s, n], z_r.at[z], zdev(to))
                cp.start()
                sends.append(cp)
        else:
            zsend[s, 0] = jnp.where(mine, back, mix).astype(BF16)
            to = z + 1 - 2 * (z % 2)
            cp = remote(zsend.at[s, 0], zrecv.at[z], z_s.at[s, 0], z_r.at[z], zdev(to))
            cp.start()
            sends.append(cp)
            total = jnp.where(mine, mix, back)

    for k in range(1, NZ):
        zz = at_z(k)
        remote(gzrecv.at[zz], gzrecv.at[zz], gz_s.at[k], gz_r.at[zz], zdev(zz)).wait_recv()
    gc_sum = gzrecv[0]
    for k in range(1, NZ):
        gc_sum = gc_sum + gzrecv[k]
    gycs[0] = gc_sum
    gy = remote(gycs.at[0], gycs.at[1], p_s.at[0], p_r.at[0], over)
    gy.start()
    for k in range(1, NZ):
        zz = at_z(k)
        remote(zsend.at[0, 0], zrecv.at[zz], z_s.at[0, 0], z_r.at[zz], zdev(zz)).wait_recv()
        total = total + zrecv[zz].astype(F32)
    ysend[...] = total.astype(BF16)
    theirs = pl.ds(pl.multiple_of(T * (1 - h), T), 2 * T)
    yc = remote(ysend.at[:, theirs], yrecv, p_s.at[1], p_r.at[1], over)
    yc.start()
    gy.wait_recv()
    gc_sum = gc_sum + gycs[1]
    gycs[2] = gc_sum
    gx = remote(gycs.at[2], gycs.at[3], p_s.at[2], p_r.at[2], twin)
    gx.start()
    yc.wait_recv()
    window = jnp.where(h == 0, total[:, 0:2 * T], total[:, T:3 * T])
    final = (window + yrecv[...].astype(F32)).astype(BF16)
    fsend[...] = final
    fc = remote(fsend, frecv, p_s.at[3], p_r.at[3], twin)
    fc.start()
    shift = 64 * h + 96 * c
    pick = (iota((2 * T, T), 0) == iota((2 * T, T), 1) + shift).astype(F32).astype(BF16)
    gx.wait_recv()
    gc_sum = gc_sum + gycs[3]
    square = jnp.concatenate([gc_sum, jnp.zeros((T - 8, T), F32)], axis=0)
    gcomb_ref[...] = square.T[:, 0:2]
    a = nn(final, pick)
    fc.wait_recv()
    b = nn(frecv[...], pick)
    mixed_ref[...] = jnp.where(mine, a, b)[:, 0:96].astype(BF16)
    gtok_ref[...] = jnp.where(mine, b, a)[:, 0:96].astype(BF16)

    for cp in sends:
        cp.wait_send()
    for cp in (xact, gy, yc, gx, fc):
        cp.wait_send()
    for cp in stores:
        cp.wait()


def local(tokens, expert_ids, combine, cotangent, w_gate, w_up, w_down):
    any_spec = pl.BlockSpec(memory_space=pl.ANY)
    vmem = pl.BlockSpec(memory_space=pltpu.VMEM)
    dma = pltpu.SemaphoreType.DMA
    mixed, gtok, gcomb, gg, gu, gd = pl.pallas_call(
        kernel,
        out_shape=(
            jax.ShapeDtypeStruct((T, 96), BF16),
            jax.ShapeDtypeStruct((T, 96), BF16),
            jax.ShapeDtypeStruct((T, 2), F32),
            jax.ShapeDtypeStruct((D, W), BF16),
            jax.ShapeDtypeStruct((D, W), BF16),
            jax.ShapeDtypeStruct((W, D), BF16),
        ),
        in_specs=[any_spec, vmem, vmem, any_spec, any_spec, any_spec, any_spec],
        out_specs=(vmem, vmem, vmem, any_spec, any_spec, any_spec),
        scratch_shapes=[
            pltpu.VMEM((2 * T, HD), BF16),
            pltpu.VMEM((D, W), BF16),
            pltpu.VMEM((D, W), BF16),
            pltpu.VMEM((W, D), BF16),
            pltpu.VMEM((NP, CH, W), BF16),
            pltpu.VMEM((NP, CH, W), BF16),
            pltpu.VMEM((NP, W, CH), BF16),
            pltpu.VMEM((NE, 2 * T), F32),
            pltpu.VMEM((NE, 2 * T), F32),
            pltpu.VMEM((NE, BLK, HD), BF16),
            pltpu.VMEM((2, NE, BLK, HD), BF16),
            pltpu.VMEM((3, NE * CAP, W), BF16),
            pltpu.VMEM((3, NE * CAP, W), BF16),
            pltpu.VMEM((NE, CAP, T), F32),
            pltpu.VMEM((NE, CAP, T), F32),
            pltpu.VMEM((3 * T, NE * BLK), BF16),
            pltpu.VMEM((NP, NE, BLK, CH), BF16),
            pltpu.VMEM((NP, NE, BLK, CH), BF16),
            pltpu.VMEM((NP, 2, T, CH), BF16),
            pltpu.VMEM((NZ, T, CH), BF16),
            pltpu.VMEM((NZ, 8, T), F32),
            pltpu.VMEM((T, CH), BF16),
            pltpu.VMEM((T, 2 * T), BF16),
            pltpu.VMEM((4, 8, T), F32),
            pltpu.VMEM((T, 2 * T), BF16),
            pltpu.VMEM((T, 2 * T), BF16),
            pltpu.VMEM((D, W), BF16),
            pltpu.VMEM((D, W), BF16),
            pltpu.VMEM((W, D), BF16),
            dma((6,)),
            dma((3,)),
            dma((3, NP)),
            dma((3, NP)),
            dma((7,)),
            dma((NE,)),
            dma((8,)),
            dma((NE,)),
            dma,
            dma,
            dma((7,)),
            dma((NE,)),
            dma((NP, 7)),
            dma((NP, NE)),
            dma((NP, 2)),
            dma((NZ,)),
            dma((NZ,)),
            dma((NZ,)),
            dma((4,)),
            dma((4,)),
        ],
        compiler_params=pltpu.CompilerParams(
            collective_id=0, has_side_effects=True, vmem_limit_bytes=60 * 1024 * 1024
        ),
        name="moe_layer",
    )(tokens, expert_ids, combine, cotangent, w_gate[0], w_up[0], w_down[0])
    return mixed, gtok, gcomb, gg[None], gu[None], gd[None]


def solution(mesh):
    in_specs = (
        P("expert", None),
        P("expert", None),
        P("expert", None),
        P("expert", None),
        P("expert", None, "dp"),
        P("expert", None, "dp"),
        P("expert", "dp", None),
    )
    out_specs = (
        P("expert", "dp"),
        P("expert", "dp"),
        P("expert", None),
        P("expert", None, "dp"),
        P("expert", None, "dp"),
        P("expert", "dp", None),
    )
    return jax.shard_map(local, mesh=mesh, in_specs=in_specs, out_specs=out_specs, check_vma=False)
```

time: 566 us -> 103 us (0.18)
  waiting for transfers between devices: 337 us -> 0 us
  blocking collectives: 126 us -> 0 us
  Pallas kernels: 0 us -> 89.2 us
  local copies, waits for them, and re-layouts: 34.3 us -> 13.1 us
  matrix products: 21 us -> 0 us
  starting transfers between devices: 14.8 us -> 0 us
  between operations: 14.9 us -> 0.65 us
  other arithmetic: 12.7 us -> 0 us
    unnamed x2 -> x0, waiting for transfers between devices: 290 us -> none
    psum x1 -> x0, blocking collectives: 126 us -> none  [local(): grad_combine = lax.psum(dot_terms, 'dp')]
    pallas_call x0 -> x1, Pallas kernels: none -> 89.2 us  [local(): pl.pallas_call(kernel, out_shape=(jax.ShapeDtypeStruct((T, 96), BF16), ja...]
    all_to_all x3 -> x0, waiting for transfers between devices: 46.4 us -> none  [the longest x1 22.7 us: local(): lax.all_to_all(x_buffer, 'expert', split_axis=0, concat_axis=0, tiled=True)]
    dot_general x9 -> x0, matrix products: 21 us -> none  [the longest x3 11.1 us: contract_rows(): lax.dot_general(left, right, (((0,), (0,)), ((), ())), preferred_element_...]
    all_to_all x3 -> x0, starting transfers between devices: 14.6 us -> none  [the longest x1 5.99 us: local(): lax.all_to_all(e_buffer, 'expert', split_axis=0, concat_axis=0, tiled=True)]
    another operation x2 -> x0, local copies, waits for them, and re-layouts: 14.2 us -> none  [the longest x1 14.2 us: local(): stacked = jnp.stack([out_part, input_part], axis=1)]
    gather x4 -> x0, local copies, waits for them, and re-layouts: 10.3 us -> none  [the longest x1 3.46 us: local(): x_buffer = jnp.where(is_live, tokens[token_of], jnp.zeros((), jnp.bfloat16))]
  transfers between devices with their start and end apart: 4 -> 0, of which waited for: 4 -> 0; matrix products, arithmetic and copies ran while one was open for 4% -> 0% of each run, Pallas kernels for 0% -> 0%
where the time goes in v1:
time: 103 us
  Pallas kernels  89.2 us (87%)
  local copies, waits for them, and re-layouts  13.1 us (13%)
    pallas_call x1, Pallas kernels, local(): pl.pallas_call(kernel, out_shape=(jax.ShapeDtypeStruct((T, 96), BF16), ja...  89.2 us
    unnamed x12, local copies, waits for them, and re-layouts  13.1 us

profile of v1, /device:TPU:1, one launch (start us, length us, event | category | flops | bytes accessed | tf_op | source)
XLA Modules:
  0.0 103.0 jit_solution(12497761442278918290)
XLA Ops:
  0.6 1.4 %copy.13.ids_ref = s32[128,2]{1,0:T(8,128)} copy(s32[128,2]{0,1:T(2,128)} %param.8) | data formatting | bytes 2048 | tf_op args[1]
  2.0 1.4 %copy.14.comb_ref = f32[128,2]{1,0:T(8,128)} copy(f32[128,2]{0,1:T(2,128)} %param.9) | data formatting | bytes 2048 | tf_op args[2]
  3.5 89.2 %moe_layer.1 = (bf16[128,96]{1,0:T(8,128)(2,1)}, bf16[128,96]{1,0:T(8,128)(2,1)}, f32[128,2]{1,0:T(8,128)}, bf16[3072,256]{1,0:T(8,128)(2,1)}, bf16[3072,256]{1,0:T(8,128)(2,1)}, /*index=5*/bf16[256,3072]{1,0:T(8,128)(2,1)}) custom-call(bf16[128,3072]{1,0:T(8,128)(2,1)} %tok_hbm.1, s32[128,2]{1,0:T(8,128)} %copy.13.ids_ref, f32[128,2]{1,0:T(8,128)} %copy.14.comb_ref, ...), custom_call_target="tpu_custom_call" | custom-call | tf_op jit(solution)/shard_map/moe_layer/pallas_call | solution.py:355
  92.7 1.5 %copy.15 = bf16[128,96]{0,1:T(8,128)(2,1)} copy(bf16[128,96]{1,0:T(8,128)(2,1)} %get-tuple-element.18) | data formatting | bytes 49152
  94.2 1.5 %copy.17 = f32[128,2]{0,1:T(2,128)} copy(f32[128,2]{1,0:T(8,128)} %get-tuple-element.20) | data formatting | bytes 2048
  95.6 1.5 %copy.16 = bf16[128,96]{0,1:T(8,128)(2,1)} copy(bf16[128,96]{1,0:T(8,128)(2,1)} %get-tuple-element.19) | data formatting | bytes 49152
  97.1 0.0 copy-start.1
  97.1 2.8 %copy.21 = bf16[1,3072,256]{2,1,0:T(8,128)(2,1)} copy(bf16[1,3072,256]{2,1,0:T(8,128)(2,1)} %bitcast.8) | data formatting | bytes 3145728
  99.9 0.0 copy-done.1
  99.9 0.0 copy-start
  99.9 1.1 %copy.22 = bf16[1,3072,256]{2,1,0:T(8,128)(2,1)} copy(bf16[1,3072,256]{2,1,0:T(8,128)(2,1)S(1)} %bitcast.7) | data formatting | bytes 3145728
  101.0 0.8 copy-done
  101.9 1.1 %copy.23 = bf16[1,256,3072]{2,1,0:T(8,128)(2,1)} copy(bf16[1,256,3072]{2,1,0:T(8,128)(2,1)S(1)} %bitcast.6) | data formatting | bytes 3145728
Async XLA Ops:
  97.1 2.8 %copy-start.1 = (bf16[3072,256]{1,0:T(8,128)(2,1)S(1)}, bf16[3072,256]{1,0:T(8,128)(2,1)}, u32[]{:S(2)}) copy-start(bf16[3072,256]{1,0:T(8,128)(2,1)} %get-tuple-element.16) | copy-start | bytes 4718596
  99.9 2.0 %copy-start = (bf16[256,3072]{1,0:T(8,128)(2,1)S(1)}, bf16[256,3072]{1,0:T(8,128)(2,1)}, u32[]{:S(2)}) copy-start(bf16[256,3072]{1,0:T(8,128)(2,1)} %get-tuple-element.17) | copy-start | bytes 4718596

commit v2 on v1

v2 whole, which is shorter than its diff:
```python
import jax
import jax.numpy as jnp
from jax import lax
from jax.experimental import pallas as pl
from jax.experimental.pallas import tpu as pltpu
from jax.sharding import PartitionSpec as P

MESH = pl.DeviceIdType.MESH
F32 = jnp.float32
BF16 = jnp.bfloat16

T = 128
D = 3072
HD = 1536
QD = 768
CAP = 40
BLK = 2 * CAP
SLAB = 48
NE = 8
NZ = 8
W = 256
CH = 384
NP = 4

FAR = (2, 1, 3, 0)

PLANE = ((2, 1), (1, 1), (3, 1), (2, 0), (0, 1), (1, 0), (3, 0))


def nn(a, b):
    return lax.dot_general(a, b, (((1,), (0,)), ((), ())), preferred_element_type=F32)


def nt(a, b):
    return lax.dot_general(a, b, (((1,), (1,)), ((), ())), preferred_element_type=F32)


def tn(a, b):
    return lax.dot_general(a, b, (((0,), (0,)), ((), ())), preferred_element_type=F32)


def iota(shape, axis):
    return lax.broadcasted_iota(jnp.int32, shape, axis)


def kernel(
    tok_hbm, ids_ref, comb_ref, cot_hbm, wg_hbm, wu_hbm, wd_hbm,
    mixed_ref, gtok_ref, gcomb_ref, gg_hbm, gu_hbm, gd_hbm,
    tc, wg, wu, wd, wgx, wux, wdx, slt, cwt, sendb, rows, acts, actx,
    gsend, grecv, tmat, rsend, rrecv, zsend, zrecv, gzrecv, ysend, yrecv, gycs,
    fsend, frecv, og, ou, od,
    lsem, osem, ws_s, ws_r, d_s, d_r, n_s, n_r, c_s, c_r, x_s, x_r, g_s, g_r, r_s, r_r,
    z_s, z_r, gz_s, gz_r, y_s, y_r, p_s, p_r,
):
    d = lax.axis_index("dp")
    e = lax.axis_index("expert")
    z, h, c = d // 4, (d // 2) % 2, d % 2
    yl, x = e // 4, e % 4
    twin = (z * 4 + h * 2 + (1 - c), e)
    over = (z * 4 + (1 - h) * 2 + c, e)

    def plane(step):
        return ((yl + step[1]) % 2) * 4 + (x + step[0]) % 4

    def at_z(k):
        return (z + k) % NZ

    def zdev(zz):
        return (zz * 4 + h * 2 + c, e)

    def remote(src, dst, ssem, rsem, dev):
        return pltpu.make_async_remote_copy(
            src_ref=src, dst_ref=dst, send_sem=ssem, recv_sem=rsem, device_id=dev, device_id_type=MESH
        )

    par = z % 2
    quarter = pl.multiple_of(c * HD + par * QD, QD)
    mate = z + 1 - 2 * par
    mate_over = (mate * 4 + (1 - h) * 2 + c, e)
    near = (zdev(mate), zdev((z + 2 * par + NZ - 1) % NZ))

    loads = [
        pltpu.make_async_copy(tok_hbm.at[:, pl.ds(quarter, QD)], tc.at[pl.ds(0, T)], lsem.at[0]),
        pltpu.make_async_copy(cot_hbm.at[:, pl.ds(quarter, QD)], tc.at[pl.ds(T, T)], lsem.at[1]),
        pltpu.make_async_copy(wg_hbm, wg, lsem.at[2]),
        pltpu.make_async_copy(wu_hbm, wu, lsem.at[3]),
        pltpu.make_async_copy(wd_hbm, wd, lsem.at[4]),
    ]
    for cp in loads:
        cp.start()

    barrier = pltpu.get_barrier_semaphore()
    for step in PLANE:
        pl.semaphore_signal(barrier, inc=1, device_id=(d, plane(step)), device_id_type=MESH)
    for k in range(1, NZ):
        pl.semaphore_signal(barrier, inc=1, device_id=zdev(at_z(k)), device_id_type=MESH)
    pl.semaphore_signal(barrier, inc=1, device_id=twin, device_id_type=MESH)
    pl.semaphore_signal(barrier, inc=1, device_id=over, device_id_type=MESH)
    pl.semaphore_signal(barrier, inc=1, device_id=mate_over, device_id_type=MESH)

    deep = iota((T, T), 0)
    lane = iota((T, T), 1)
    ids = ids_ref[...]
    comb = comb_ref[...]
    pick0 = deep == ids[0:1]
    pick1 = deep == ids[1:2]
    chosen = jnp.logical_or(pick0, pick1)
    earlier = (deep < lane).astype(F32).astype(BF16)
    rank = nn(chosen.astype(F32).astype(BF16), earlier)
    slot = jnp.where(chosen, rank, -128.0)
    weight = jnp.where(pick0, comb[0:1], 0.0) + jnp.where(pick1, comb[1:2], 0.0)
    slt[...] = jnp.concatenate([slot[0:NE], slot[0:NE]], axis=1)
    cwt[...] = jnp.concatenate([jnp.ones((NE, T), F32), weight[0:NE]], axis=1)

    loads[0].wait()
    loads[1].wait()
    pl.semaphore_wait(barrier, len(PLANE) + NZ - 1 + 3)

    def pack(j):
        slots = slt[pl.ds(j, 1), :]
        weights = cwt[pl.ds(j, 1), :]
        row = iota((BLK, 2 * T), 0)
        col = iota((BLK, 2 * T), 1)
        want = jnp.where(col < T, row, row - CAP).astype(F32)
        hit = want == slots
        scale = jnp.sum(jnp.where(hit, weights, 0.0), axis=1, keepdims=True)
        block = nn(hit.astype(F32).astype(BF16), tc[...])
        sendb[j] = (block * scale).astype(BF16)

    sends = []
    for i, step in enumerate(PLANE):
        j = plane(step)
        pack(j)
        cp = remote(sendb.at[j], rows.at[c, par, e], d_s.at[i], d_r.at[e], (d, j))
        cp.start()
        sends.append(cp)
    pack(e)
    def spread(i, j, src):
        for n in range(2):
            part = pl.ds(n * CH, CH)
            cp = remote(src.at[:, part], rows.at[c, par, j, :, part], n_s.at[n, i], n_r.at[n, j], near[n])
            cp.start()
            sends.append(cp)
        cp = remote(src, rows.at[c, par, j], c_s.at[0, i], c_r.at[0, j], twin)
        cp.start()
        sends.append(cp)

    spread(7, e, sendb.at[e])
    own = pltpu.make_async_copy(sendb.at[e], rows.at[c, par, e], lsem.at[5])
    own.start()

    for m in range(NP):
        for n, (src, dst) in enumerate((
            (wd_hbm.at[:, pl.ds(pl.multiple_of((2 * m + 1 - c) * CH, CH), CH)], wdx.at[m]),
            (wg_hbm.at[pl.ds(pl.multiple_of((2 * m + c) * CH, CH), CH)], wgx.at[m]),
            (wu_hbm.at[pl.ds(pl.multiple_of((2 * m + c) * CH, CH), CH)], wux.at[m]),
        )):
            cp = remote(src, dst, ws_s.at[n, m], ws_r.at[n, m], twin)
            cp.start()
            sends.append(cp)

    expand = (iota((T, NE * BLK), 0) == iota((T, NE * BLK), 1) // BLK).astype(F32).astype(BF16)
    weight_t = weight.T
    w_hi = weight_t.astype(BF16)
    w_lo = (weight_t - w_hi.astype(F32)).astype(BF16)
    inner = (iota((T, NE * BLK), 1) % BLK).astype(F32)
    slots_all = nn(slot.T.astype(BF16), expand)
    out_hit = slots_all == inner
    tmat[0:T] = jnp.where(out_hit, nn(w_hi, expand), 0.0).astype(BF16)
    tmat[T:2 * T] = jnp.where(out_hit, nn(w_lo, expand), 0.0).astype(BF16)
    tmat[2 * T:3 * T] = (slots_all == inner - CAP).astype(F32).astype(BF16)

    for i, step in enumerate(PLANE):
        j = plane((4 - step[0], step[1]))
        here = rows.at[c, par, j]
        remote(here, here, d_s.at[i], d_r.at[j], (d, j)).wait_recv()
        spread(i, j, here)
    own.wait()
    for cp in loads[2:]:
        cp.wait()

    def x_rows(cc, pp):
        return rows[cc, pp, :, 0:SLAB, :].reshape(NE * SLAB, QD)

    def e_rows(cc, pp):
        return rows[cc, pp, :, BLK - SLAB:BLK, :].reshape(NE * SLAB, QD)

    def products(cc, pp):
        at = pl.ds(pl.multiple_of(cc * HD + pp * QD, QD), QD)
        xs = x_rows(cc, pp)
        return nn(xs, wg[at, :]), nn(xs, wu[at, :]), nt(e_rows(cc, pp), wd[:, at])

    def first(a):
        return a.reshape(NE, SLAB, W)[:, 0:CAP].reshape(NE * CAP, W)

    def last(a):
        return a.reshape(NE, SLAB, W)[:, SLAB - CAP:].reshape(NE * CAP, W)

    sum3 = products(c, par)
    for i, step in enumerate(((0, 0),) + PLANE):
        j = plane((4 - step[0], step[1]))
        there = rows.at[c, 1 - par, j]
        for n in range(2):
            part = there.at[:, pl.ds(n * CH, CH)]
            remote(part, part, n_s.at[n, i], n_r.at[n, j], near[n]).wait_recv()
        cp = remote(there, there, c_s.at[1, i], c_r.at[1, j], twin)
        cp.start()
        sends.append(cp)
    for n, pp in enumerate((par, 1 - par)):
        for i, step in enumerate(((0, 0),) + PLANE):
            j = plane((4 - step[0], step[1]))
            there = rows.at[1 - c, pp, j]
            remote(there, there, c_s.at[n, i], c_r.at[n, j], twin).wait_recv()
        if n == 0:
            sum3 = [u + v for u, v in zip(sum3, products(1 - c, par))]
            sum3 = [u + v for u, v in zip(sum3, products(c, 1 - par))]
        else:
            sum3 = [u + v for u, v in zip(sum3, products(1 - c, 1 - par))]
    gate, up, hgrad = first(sum3[0]), first(sum3[1]), last(sum3[2])
    sig = jax.nn.sigmoid(gate)
    active = gate * sig
    hidden = (active * up).astype(BF16)
    gate_grad = (hgrad * up * sig * (1.0 + gate * (1.0 - sig))).astype(BF16)
    up_grad = (hgrad * active).astype(BF16)
    acts[0] = hidden
    acts[1] = gate_grad
    acts[2] = up_grad
    xact = remote(acts, actx, x_s, x_r, twin)
    xact.start()
    hid32 = hidden.astype(F32)
    dots = jnp.sum(hid32 * hgrad, axis=1, keepdims=True)
    gsend[...] = jnp.broadcast_to(dots, (NE * CAP, T)).reshape(NE, CAP, T)
    for i, step in enumerate(PLANE):
        j = plane(step)
        cp = remote(gsend.at[j], grecv.at[e], g_s.at[i], g_r.at[e], (d, j))
        cp.start()
        sends.append(cp)
    grecv[e] = gsend[e]
    for n in range(3):
        for m in range(NP):
            cp = remote(
                (wdx, wgx, wux)[n].at[m], (wdx, wgx, wux)[n].at[m], ws_s.at[n, m], ws_r.at[n, m], twin
            )
            cp.wait_recv()
    xact.wait_recv()

    for s in range(NP):
        m = (z // 2 + FAR[s]) % NP
        oc = pl.multiple_of((2 * m + c) * CH, CH)
        tcol = pl.multiple_of((2 * m + 1 - c) * CH, CH)
        out = nn(acts[0], wd[:, pl.ds(oc, CH)]) + nn(actx[0], wdx[m])
        back = (
            nt(acts[1], wg[pl.ds(tcol, CH), :]) + nt(acts[2], wu[pl.ds(tcol, CH), :])
            + nt(actx[1], wgx[m]) + nt(actx[2], wux[m])
        )
        both = jnp.concatenate([out.reshape(NE, CAP, CH), back.reshape(NE, CAP, CH)], axis=1)
        rsend[s] = both.astype(BF16)
        for i, step in enumerate(PLANE):
            j = plane(step)
            cp = remote(rsend.at[s, j], rrecv.at[s, e], r_s.at[s, i], r_r.at[s, e], (d, j))
            cp.start()
            sends.append(cp)
        rrecv[s, e] = rsend[s, e]

    for step in PLANE:
        j = plane((4 - step[0], step[1]))
        remote(gsend.at[j], grecv.at[j], g_s.at[0], g_r.at[j], (d, j)).wait_recv()
    q = iota((NE * CAP, T), 0).astype(F32)
    values = grecv[...].reshape(NE * CAP, T)

    def gathered(pick, c_row):
        place = jnp.sum(jnp.where(pick, deep.astype(F32) * CAP + rank, 0.0), axis=0, keepdims=True)
        return jnp.sum(jnp.where(q == place, values, 0.0), axis=0, keepdims=True) / c_row

    sub = iota((8, T), 0)
    gzrecv[z] = jnp.where(
        sub == 0, gathered(pick0, comb[0:1]), jnp.where(sub == 1, gathered(pick1, comb[1:2]), 0.0)
    )
    for k in range(1, NZ):
        cp = remote(gzrecv.at[z], gzrecv.at[z], gz_s.at[k], gz_r.at[z], zdev(at_z(k)))
        cp.start()
        sends.append(cp)

    def padded(a, lead):
        a = a.astype(F32).reshape(NE, CAP, W)
        zero = jnp.zeros((NE, SLAB - CAP, W), F32)
        a = jnp.concatenate([a, zero] if lead else [zero, a], axis=1)
        return a.reshape(NE * SLAB, W).astype(BF16)

    hid_pad = padded(acts[0], False)
    pair_pad = jnp.concatenate([padded(acts[1], True), padded(acts[2], True)], axis=1)
    stores = []

    def weight_grads(k):
        at = k * QD
        both = tn(x_rows(k // 2, k % 2), pair_pad)
        og[at:at + QD] = both[:, 0:W].astype(BF16)
        ou[at:at + QD] = both[:, W:2 * W].astype(BF16)
        od[:, at:at + QD] = tn(hid_pad, e_rows(k // 2, k % 2)).astype(BF16)
        for n, (src, dst) in enumerate((
            (og.at[pl.ds(at, QD)], gg_hbm.at[pl.ds(at, QD)]),
            (ou.at[pl.ds(at, QD)], gu_hbm.at[pl.ds(at, QD)]),
            (od.at[:, pl.ds(at, QD)], gd_hbm.at[:, pl.ds(at, QD)]),
        )):
            cp = pltpu.make_async_copy(src, dst, osem.at[n, k])
            cp.start()
            stores.append(cp)

    mine = par == c
    windows = [pl.ds(pl.multiple_of(T * hh, T), 2 * T) for hh in (h, 1 - h)]
    for s in range(NP):
        weight_grads(s)
        for step in PLANE:
            j = plane((4 - step[0], step[1]))
            remote(rsend.at[s, j], rrecv.at[s, j], r_s.at[s, 0], r_r.at[s, j], (d, j)).wait_recv()
        m = (z // 2 + FAR[s]) % NP
        sums = nn(tmat[...], rrecv[s].reshape(NE * BLK, CH))
        mix = sums[0:T] + sums[T:2 * T]
        back = sums[2 * T:3 * T]
        if s < NP - 1:
            zsend[s, 0] = mix.astype(BF16)
            zsend[s, 1] = back.astype(BF16)
            for n in range(2):
                to = 2 * m + (c if n == 0 else 1 - c)
                cp = remote(zsend.at[s, n], zrecv.at[z], z_s.at[s, n], z_r.at[z], zdev(to))
                cp.start()
                sends.append(cp)
        else:
            zsend[s, 0] = jnp.where(mine, back, mix).astype(BF16)
            for n, (src, dev) in enumerate((
                (zsend.at[s, 0, :, windows[0]], zdev(mate)),
                (zsend.at[s, 0, :, windows[1]], mate_over),
            )):
                cp = remote(src, yrecv.at[n], y_s.at[n], y_r.at[n], dev)
                cp.start()
                sends.append(cp)
            total = jnp.where(mine, mix, back)
    for k in FAR[:NP - 1]:
        for n in range(2):
            zz = 2 * ((z // 2 + NP - k) % NP) + n
            remote(zsend.at[0, 0], zrecv.at[zz], z_s.at[0, 0], z_r.at[zz], zdev(zz)).wait_recv()
            total = total + zrecv[zz].astype(F32)
    ysend[...] = total.astype(BF16)
    yc = remote(ysend.at[:, windows[1]], yrecv.at[2], y_s.at[2], y_r.at[2], over)
    yc.start()
    for k in range(1, NZ):
        zz = at_z(k)
        remote(gzrecv.at[zz], gzrecv.at[zz], gz_s.at[k], gz_r.at[zz], zdev(zz)).wait_recv()
    gc_sum = gzrecv[0]
    for k in range(1, NZ):
        gc_sum = gc_sum + gzrecv[k]
    gycs[0] = gc_sum
    gy = remote(gycs.at[0], gycs.at[1], p_s.at[0], p_r.at[0], over)
    gy.start()
    gy.wait_recv()
    gc_sum = gc_sum + gycs[1]
    gycs[2] = gc_sum
    gx = remote(gycs.at[2], gycs.at[3], p_s.at[1], p_r.at[1], twin)
    gx.start()
    for n in range(3):
        remote(yrecv.at[n], yrecv.at[n], y_s.at[n], y_r.at[n], over).wait_recv()
    window = jnp.where(h == 0, total[:, 0:2 * T], total[:, T:3 * T])
    window = window + yrecv[0].astype(F32) + yrecv[1].astype(F32) + yrecv[2].astype(F32)
    final = window.astype(BF16)
    fsend[...] = final
    fc = remote(fsend, frecv, p_s.at[2], p_r.at[2], twin)
    fc.start()
    shift = 64 * h + 96 * c
    pick = (iota((T, 2 * T), 1) == iota((T, 2 * T), 0) + shift).astype(F32).astype(BF16)
    gx.wait_recv()
    gc_sum = gc_sum + gycs[3]
    gcomb_ref[...] = gc_sum[0:2]
    a = nt(pick, final)
    fc.wait_recv()
    b = nt(pick, frecv[...])
    mixed_ref[...] = jnp.where(mine, a, b)[0:96].astype(BF16)
    gtok_ref[...] = jnp.where(mine, b, a)[0:96].astype(BF16)

    for cp in sends:
        cp.wait_send()
    for cp in (xact, gy, yc, gx, fc):
        cp.wait_send()
    for cp in stores:
        cp.wait()


def settle_kernel(*refs):
    sources, targets, held, came, went = refs[0:6], refs[6:12], refs[12:18], refs[18], refs[19]
    moves = []
    for i in range(6):
        rows = sources[i].shape[0]
        parts = 4 if rows * sources[i].shape[1] > T * T else 1
        for k in range(parts):
            cut = pl.ds(k * (rows // parts), rows // parts)
            moves.append((i, k, cut))
    ins = [pltpu.make_async_copy(sources[i].at[cut], held[i].at[cut], came.at[i, k]) for i, k, cut in moves]
    outs = [pltpu.make_async_copy(held[i].at[cut], targets[i].at[cut], went.at[i, k]) for i, k, cut in moves]
    for cp in ins:
        cp.start()
    for come, go in zip(ins, outs):
        come.wait()
        go.start()
    for cp in outs:
        cp.wait()


def settle(*arrays):
    any_spec = pl.BlockSpec(memory_space=pl.ANY)
    return pl.pallas_call(
        settle_kernel,
        out_shape=tuple(jax.ShapeDtypeStruct(a.shape, a.dtype) for a in arrays),
        in_specs=[any_spec] * 6,
        out_specs=(any_spec,) * 6,
        scratch_shapes=[pltpu.VMEM(a.shape, a.dtype) for a in arrays]
        + [pltpu.SemaphoreType.DMA((6, 4)), pltpu.SemaphoreType.DMA((6, 4))],
        compiler_params=pltpu.CompilerParams(vmem_limit_bytes=60 * 1024 * 1024),
        name="settle",
    )(*arrays)


def local(tokens, expert_ids, combine, cotangent, w_gate, w_up, w_down):
    any_spec = pl.BlockSpec(memory_space=pl.ANY)
    vmem = pl.BlockSpec(memory_space=pltpu.VMEM)
    dma = pltpu.SemaphoreType.DMA
    mixed, gtok, gcomb, gg, gu, gd = pl.pallas_call(
        kernel,
        out_shape=(
            jax.ShapeDtypeStruct((96, T), BF16),
            jax.ShapeDtypeStruct((96, T), BF16),
            jax.ShapeDtypeStruct((2, T), F32),
            jax.ShapeDtypeStruct((D, W), BF16),
            jax.ShapeDtypeStruct((D, W), BF16),
            jax.ShapeDtypeStruct((W, D), BF16),
        ),
        in_specs=[any_spec, vmem, vmem, any_spec, any_spec, any_spec, any_spec],
        out_specs=(vmem, vmem, vmem, any_spec, any_spec, any_spec),
        scratch_shapes=[
            pltpu.VMEM((2 * T, QD), BF16),
            pltpu.VMEM((D, W), BF16),
            pltpu.VMEM((D, W), BF16),
            pltpu.VMEM((W, D), BF16),
            pltpu.VMEM((NP, CH, W), BF16),
            pltpu.VMEM((NP, CH, W), BF16),
            pltpu.VMEM((NP, W, CH), BF16),
            pltpu.VMEM((NE, 2 * T), F32),
            pltpu.VMEM((NE, 2 * T), F32),
            pltpu.VMEM((NE, BLK, QD), BF16),
            pltpu.VMEM((2, 2, NE, BLK, QD), BF16),
            pltpu.VMEM((3, NE * CAP, W), BF16),
            pltpu.VMEM((3, NE * CAP, W), BF16),
            pltpu.VMEM((NE, CAP, T), F32),
            pltpu.VMEM((NE, CAP, T), F32),
            pltpu.VMEM((3 * T, NE * BLK), BF16),
            pltpu.VMEM((NP, NE, BLK, CH), BF16),
            pltpu.VMEM((NP, NE, BLK, CH), BF16),
            pltpu.VMEM((NP, 2, T, CH), BF16),
            pltpu.VMEM((NZ, T, CH), BF16),
            pltpu.VMEM((NZ, 8, T), F32),
            pltpu.VMEM((T, CH), BF16),
            pltpu.VMEM((3, T, 2 * T), BF16),
            pltpu.VMEM((4, 8, T), F32),
            pltpu.VMEM((T, 2 * T), BF16),
            pltpu.VMEM((T, 2 * T), BF16),
            pltpu.VMEM((D, W), BF16),
            pltpu.VMEM((D, W), BF16),
            pltpu.VMEM((W, D), BF16),
            dma((6,)),
            dma((3, 4)),
            dma((3, NP)),
            dma((3, NP)),
            dma((7,)),
            dma((NE,)),
            dma((2, 8)),
            dma((2, NE)),
            dma((2, 8)),
            dma((2, NE)),
            dma,
            dma,
            dma((7,)),
            dma((NE,)),
            dma((NP, 7)),
            dma((NP, NE)),
            dma((NP, 2)),
            dma((NZ,)),
            dma((NZ,)),
            dma((NZ,)),
            dma((3,)),
            dma((3,)),
            dma((3,)),
            dma((3,)),
        ],
        compiler_params=pltpu.CompilerParams(
            collective_id=0, has_side_effects=True, vmem_limit_bytes=60 * 1024 * 1024
        ),
        name="moe_layer",
    )(tokens, expert_ids.T, combine.T, cotangent, w_gate[0], w_up[0], w_down[0])
    mixed, gtok, gcomb, gg, gu, gd = settle(mixed, gtok, gcomb, gg, gu, gd)
    return mixed.T, gtok.T, gcomb.T, gg[None], gu[None], gd[None]


def solution(mesh):
    in_specs = (
        P("expert", None),
        P("expert", None),
        P("expert", None),
        P("expert", None),
        P("expert", None, "dp"),
        P("expert", None, "dp"),
        P("expert", "dp", None),
    )
    out_specs = (
        P("expert", "dp"),
        P("expert", "dp"),
        P("expert", None),
        P("expert", None, "dp"),
        P("expert", None, "dp"),
        P("expert", "dp", None),
    )
    return jax.shard_map(local, mesh=mesh, in_specs=in_specs, out_specs=out_specs, check_vma=False)
```

time: 103 us -> 79.8 us (0.77)
  local copies, waits for them, and re-layouts: 13.1 us -> 0 us
  Pallas kernels: 89.2 us -> 78.8 us
    unnamed x12 -> x0, local copies, waits for them, and re-layouts: 13.1 us -> none
    pallas_call x1 -> x2, Pallas kernels: 89.2 us -> 78.8 us  [the longest x1 74.2 us: local(): pl.pallas_call(kernel, out_shape=(jax.ShapeDtypeStruct((96, T), BF16), ja...]
where the time goes in v2:
time: 79.8 us; the launch traced here: 79.4 us
  Pallas kernels  78.8 us (99%)
    pallas_call x1, Pallas kernels, local(): pl.pallas_call(kernel, out_shape=(jax.ShapeDtypeStruct((96, T), BF16), ja...  74.2 us
    pallas_call x1, Pallas kernels, settle(): pl.pallas_call(settle_kernel, out_shape=tuple((jax.ShapeDtypeStruct(a.sha...  4.57 us

profile of v2, /device:TPU:1, one launch (start us, length us, event | category | flops | bytes accessed | tf_op | source)
XLA Modules:
  0.0 79.4 jit_solution(15603583887179189758)
XLA Ops:
  0.6 74.2 %moe_layer.1 = (bf16[96,128]{1,0:T(8,128)(2,1)}, bf16[96,128]{1,0:T(8,128)(2,1)}, f32[2,128]{1,0:T(2,128)}, bf16[3072,256]{1,0:T(8,128)(2,1)}, bf16[3072,256]{1,0:T(8,128)(2,1)}, /*index=5*/bf16[256,3072]{1,0:T(8,128)(2,1)}) custom-call(bf16[128,3072]{1,0:T(8,128)(2,1)} %tok_hbm.1, s32[2,128]{1,0:T(2,128)} %bitcast.14, f32[2,128]{1,0:T(2,128)} %bitcast.15, ...), custom_call_target="tpu_custom_call" | custom-call | tf_op jit(solution)/shard_map/moe_layer/pallas_call | solution.py:425
  74.9 4.6 %settle.1 = (bf16[96,128]{1,0:T(8,128)(2,1)}, bf16[96,128]{1,0:T(8,128)(2,1)}, f32[2,128]{1,0:T(2,128)}, bf16[3072,256]{1,0:T(8,128)(2,1)}, bf16[3072,256]{1,0:T(8,128)(2,1)}, /*index=5*/bf16[256,3072]{1,0:T(8,128)(2,1)}) custom-call(bf16[96,128]{1,0:T(8,128)(2,1)} %get-tuple-element.18.refs_0_, bf16[96,128]{1,0:T(8,128)(2,1)} %get-tuple-element.19.refs_1_, ...), custom_call_target="tpu_custom_call" | custom-call | tf_op jit(solution)/shard_map/settle/pallas_call | solution.py:409

commit v3 on v2

--- a/solution.py
+++ b/solution.py
@@ -22,7 +22,7 @@
 CH = 384
 NP = 4
 
-FAR = (2, 1, 3, 0)
+FAR = ((4, 1), (2, 5), (6, 3), (0, 7))
 
 PLANE = ((2, 1), (1, 1), (3, 1), (2, 0), (0, 1), (1, 0), (3, 0))
 
@@ -45,11 +45,11 @@
 
 def kernel(
     tok_hbm, ids_ref, comb_ref, cot_hbm, wg_hbm, wu_hbm, wd_hbm,
-    mixed_ref, gtok_ref, gcomb_ref, gg_hbm, gu_hbm, gd_hbm,
+    mixed_ref, gtok_ref, gcomb_ref, og, ou, od,
     tc, wg, wu, wd, wgx, wux, wdx, slt, cwt, sendb, rows, acts, actx,
     gsend, grecv, tmat, rsend, rrecv, zsend, zrecv, gzrecv, ysend, yrecv, gycs,
-    fsend, frecv, og, ou, od,
-    lsem, osem, ws_s, ws_r, d_s, d_r, n_s, n_r, c_s, c_r, x_s, x_r, g_s, g_r, r_s, r_r,
+    fsend, frecv,
+    lsem, ws_s, ws_r, d_s, d_r, n_s, n_r, c_s, c_r, x_s, x_r, g_s, g_r, r_s, r_r,
     z_s, z_r, gz_s, gz_r, y_s, y_r, p_s, p_r,
 ):
     d = lax.axis_index("dp")
@@ -75,9 +75,11 @@
 
     par = z % 2
     quarter = pl.multiple_of(c * HD + par * QD, QD)
-    mate = z + 1 - 2 * par
-    mate_over = (mate * 4 + (1 - h) * 2 + c, e)
-    near = (zdev(mate), zdev((z + 2 * par + NZ - 1) % NZ))
+    mine = par == c
+    below = at_z(NZ - 1)
+    below_over = (below * 4 + (1 - h) * 2 + c, e)
+    above_over = (at_z(1) * 4 + (1 - h) * 2 + c, e)
+    near = (zdev(z + 1 - 2 * par), zdev((z + 2 * par + NZ - 1) % NZ))
 
     loads = [
         pltpu.make_async_copy(tok_hbm.at[:, pl.ds(quarter, QD)], tc.at[pl.ds(0, T)], lsem.at[0]),
@@ -96,7 +98,8 @@
         pl.semaphore_signal(barrier, inc=1, device_id=zdev(at_z(k)), device_id_type=MESH)
     pl.semaphore_signal(barrier, inc=1, device_id=twin, device_id_type=MESH)
     pl.semaphore_signal(barrier, inc=1, device_id=over, device_id_type=MESH)
-    pl.semaphore_signal(barrier, inc=1, device_id=mate_over, device_id_type=MESH)
+    pl.semaphore_signal(barrier, inc=1, device_id=below_over, device_id_type=MESH)
+    pl.semaphore_signal(barrier, inc=1, device_id=above_over, device_id_type=MESH)
 
     deep = iota((T, T), 0)
     lane = iota((T, T), 1)
@@ -114,7 +117,6 @@
 
     loads[0].wait()
     loads[1].wait()
-    pl.semaphore_wait(barrier, len(PLANE) + NZ - 1 + 3)
 
     def pack(j):
         slots = slt[pl.ds(j, 1), :]
@@ -131,6 +133,8 @@
     for i, step in enumerate(PLANE):
         j = plane(step)
         pack(j)
+        if i == 0:
+            pl.semaphore_wait(barrier, len(PLANE) + NZ - 1 + 4)
         cp = remote(sendb.at[j], rows.at[c, par, e], d_s.at[i], d_r.at[e], (d, j))
         cp.start()
         sends.append(cp)
@@ -236,23 +240,30 @@
         cp.start()
         sends.append(cp)
     grecv[e] = gsend[e]
+
+    def targets(s):
+        even, odd = at_z(FAR[s][0]), at_z(FAR[s][1])
+        return jnp.where(mine, even, odd), jnp.where(mine, odd, even)
+
+    def own_sums(s):
+        to_out, to_back = targets(s)
+        oc = pl.multiple_of(to_out * CH, CH)
+        tcol = pl.multiple_of(to_back * CH, CH)
+        out = nn(acts[0], wd[:, pl.ds(oc, CH)])
+        return out, nt(acts[1], wg[pl.ds(tcol, CH), :]) + nt(acts[2], wu[pl.ds(tcol, CH), :])
+
+    start = own_sums(0)
     for n in range(3):
         for m in range(NP):
-            cp = remote(
-                (wdx, wgx, wux)[n].at[m], (wdx, wgx, wux)[n].at[m], ws_s.at[n, m], ws_r.at[n, m], twin
-            )
-            cp.wait_recv()
+            there = (wdx, wgx, wux)[n].at[m]
+            remote(there, there, ws_s.at[n, m], ws_r.at[n, m], twin).wait_recv()
     xact.wait_recv()
 
     for s in range(NP):
-        m = (z // 2 + FAR[s]) % NP
-        oc = pl.multiple_of((2 * m + c) * CH, CH)
-        tcol = pl.multiple_of((2 * m + 1 - c) * CH, CH)
-        out = nn(acts[0], wd[:, pl.ds(oc, CH)]) + nn(actx[0], wdx[m])
-        back = (
-            nt(acts[1], wg[pl.ds(tcol, CH), :]) + nt(acts[2], wu[pl.ds(tcol, CH), :])
-            + nt(actx[1], wgx[m]) + nt(actx[2], wux[m])
-        )
+        to_out, to_back = targets(s)
+        out, back = own_sums(s) if s else start
+        out = out + nn(actx[0], wdx[to_out // 2])
+        back = back + nt(actx[1], wgx[to_back // 2]) + nt(actx[2], wux[to_back // 2])
         both = jnp.concatenate([out.reshape(NE, CAP, CH), back.reshape(NE, CAP, CH)], axis=1)
         rsend[s] = both.astype(BF16)
         for i, step in enumerate(PLANE):
@@ -289,31 +300,19 @@
 
     hid_pad = padded(acts[0], False)
     pair_pad = jnp.concatenate([padded(acts[1], True), padded(acts[2], True)], axis=1)
-    stores = []
-
     def weight_grads(k):
         at = k * QD
         both = tn(x_rows(k // 2, k % 2), pair_pad)
         og[at:at + QD] = both[:, 0:W].astype(BF16)
         ou[at:at + QD] = both[:, W:2 * W].astype(BF16)
         od[:, at:at + QD] = tn(hid_pad, e_rows(k // 2, k % 2)).astype(BF16)
-        for n, (src, dst) in enumerate((
-            (og.at[pl.ds(at, QD)], gg_hbm.at[pl.ds(at, QD)]),
-            (ou.at[pl.ds(at, QD)], gu_hbm.at[pl.ds(at, QD)]),
-            (od.at[:, pl.ds(at, QD)], gd_hbm.at[:, pl.ds(at, QD)]),
-        )):
-            cp = pltpu.make_async_copy(src, dst, osem.at[n, k])
-            cp.start()
-            stores.append(cp)
-
-    mine = par == c
+
     windows = [pl.ds(pl.multiple_of(T * hh, T), 2 * T) for hh in (h, 1 - h)]
     for s in range(NP):
         weight_grads(s)
         for step in PLANE:
             j = plane((4 - step[0], step[1]))
             remote(rsend.at[s, j], rrecv.at[s, j], r_s.at[s, 0], r_r.at[s, j], (d, j)).wait_recv()
-        m = (z // 2 + FAR[s]) % NP
         sums = nn(tmat[...], rrecv[s].reshape(NE * BLK, CH))
         mix = sums[0:T] + sums[T:2 * T]
         back = sums[2 * T:3 * T]
@@ -321,15 +320,14 @@
             zsend[s, 0] = mix.astype(BF16)
             zsend[s, 1] = back.astype(BF16)
             for n in range(2):
-                to = 2 * m + (c if n == 0 else 1 - c)
-                cp = remote(zsend.at[s, n], zrecv.at[z], z_s.at[s, n], z_r.at[z], zdev(to))
+                cp = remote(zsend.at[s, n], zrecv.at[z], z_s.at[s, n], z_r.at[z], zdev(targets(s)[n]))
                 cp.start()
                 sends.append(cp)
         else:
             zsend[s, 0] = jnp.where(mine, back, mix).astype(BF16)
             for n, (src, dev) in enumerate((
-                (zsend.at[s, 0, :, windows[0]], zdev(mate)),
-                (zsend.at[s, 0, :, windows[1]], mate_over),
+                (zsend.at[s, 0, :, windows[0]], zdev(below)),
+                (zsend.at[s, 0, :, windows[1]], below_over),
             )):
                 cp = remote(src, yrecv.at[n], y_s.at[n], y_r.at[n], dev)
                 cp.start()
@@ -337,7 +335,7 @@
             total = jnp.where(mine, mix, back)
     for k in FAR[:NP - 1]:
         for n in range(2):
-            zz = 2 * ((z // 2 + NP - k) % NP) + n
+            zz = at_z(NZ - k[n])
             remote(zsend.at[0, 0], zrecv.at[zz], z_s.at[0, 0], z_r.at[zz], zdev(zz)).wait_recv()
             total = total + zrecv[zz].astype(F32)
     ysend[...] = total.astype(BF16)
@@ -380,27 +378,13 @@
         cp.wait_send()
     for cp in (xact, gy, yc, gx, fc):
         cp.wait_send()
-    for cp in stores:
-        cp.wait()
 
 
 def settle_kernel(*refs):
-    sources, targets, held, came, went = refs[0:6], refs[6:12], refs[12:18], refs[18], refs[19]
-    moves = []
-    for i in range(6):
-        rows = sources[i].shape[0]
-        parts = 4 if rows * sources[i].shape[1] > T * T else 1
-        for k in range(parts):
-            cut = pl.ds(k * (rows // parts), rows // parts)
-            moves.append((i, k, cut))
-    ins = [pltpu.make_async_copy(sources[i].at[cut], held[i].at[cut], came.at[i, k]) for i, k, cut in moves]
-    outs = [pltpu.make_async_copy(held[i].at[cut], targets[i].at[cut], went.at[i, k]) for i, k, cut in moves]
-    for cp in ins:
-        cp.start()
-    for come, go in zip(ins, outs):
-        come.wait()
-        go.start()
-    for cp in outs:
+    copies = [pltpu.make_async_copy(refs[i], refs[6 + i], refs[12].at[i]) for i in range(6)]
+    for cp in copies:
+        cp.start()
+    for cp in copies:
         cp.wait()
 
 
@@ -411,9 +395,8 @@
         out_shape=tuple(jax.ShapeDtypeStruct(a.shape, a.dtype) for a in arrays),
         in_specs=[any_spec] * 6,
         out_specs=(any_spec,) * 6,
-        scratch_shapes=[pltpu.VMEM(a.shape, a.dtype) for a in arrays]
-        + [pltpu.SemaphoreType.DMA((6, 4)), pltpu.SemaphoreType.DMA((6, 4))],
-        compiler_params=pltpu.CompilerParams(vmem_limit_bytes=60 * 1024 * 1024),
+        scratch_shapes=[pltpu.SemaphoreType.DMA((6,))],
+        compiler_params=pltpu.CompilerParams(vmem_limit_bytes=16 * 1024 * 1024),
         name="settle",
     )(*arrays)
 
@@ -425,15 +408,15 @@
     mixed, gtok, gcomb, gg, gu, gd = pl.pallas_call(
         kernel,
         out_shape=(
-            jax.ShapeDtypeStruct((96, T), BF16),
-            jax.ShapeDtypeStruct((96, T), BF16),
-            jax.ShapeDtypeStruct((2, T), F32),
-            jax.ShapeDtypeStruct((D, W), BF16),
-            jax.ShapeDtypeStruct((D, W), BF16),
-            jax.ShapeDtypeStruct((W, D), BF16),
+            pltpu.VMEM((96, T), BF16),
+            pltpu.VMEM((96, T), BF16),
+            pltpu.VMEM((2, T), F32),
+            pltpu.VMEM((D, W), BF16),
+            pltpu.VMEM((D, W), BF16),
+            pltpu.VMEM((W, D), BF16),
         ),
         in_specs=[any_spec, vmem, vmem, any_spec, any_spec, any_spec, any_spec],
-        out_specs=(vmem, vmem, vmem, any_spec, any_spec, any_spec),
+        out_specs=(vmem,) * 6,
         scratch_shapes=[
             pltpu.VMEM((2 * T, QD), BF16),
             pltpu.VMEM((D, W), BF16),
@@ -461,11 +444,7 @@
             pltpu.VMEM((4, 8, T), F32),
             pltpu.VMEM((T, 2 * T), BF16),
             pltpu.VMEM((T, 2 * T), BF16),
-            pltpu.VMEM((D, W), BF16),
-            pltpu.VMEM((D, W), BF16),
-            pltpu.VMEM((W, D), BF16),
             dma((6,)),
-            dma((3, 4)),
             dma((3, NP)),
             dma((3, NP)),
             dma((7,)),
@@ -490,7 +469,7 @@
             dma((3,)),
         ],
         compiler_params=pltpu.CompilerParams(
-            collective_id=0, has_side_effects=True, vmem_limit_bytes=60 * 1024 * 1024
+            collective_id=0, has_side_effects=True, vmem_limit_bytes=59 * 1024 * 1024
         ),
         name="moe_layer",
     )(tokens, expert_ids.T, combine.T, cotangent, w_gate[0], w_up[0], w_down[0])

time: 79.8 us -> 75.9 us (0.951)
  Pallas kernels: 78.8 us -> 75 us
    pallas_call x1, Pallas kernels: 4.57 us -> 2.25 us  [settle(): pl.pallas_call(settle_kernel, out_shape=tuple((jax.ShapeDtypeStruct(a.sha...]
    pallas_call x1, Pallas kernels: 74.2 us -> 72.7 us  [local(): pl.pallas_call(kernel, out_shape=(pltpu.VMEM((96, T), BF16), pltpu.VMEM((...]
where the time goes in v3:
time: 75.9 us; the launch traced here: 75.6 us
  Pallas kernels  75 us (99%)
    pallas_call x1, Pallas kernels, local(): pl.pallas_call(kernel, out_shape=(pltpu.VMEM((96, T), BF16), pltpu.VMEM((...  72.7 us
    pallas_call x1, Pallas kernels, settle(): pl.pallas_call(settle_kernel, out_shape=tuple((jax.ShapeDtypeStruct(a.sha...  2.25 us

profile of v3, /device:TPU:1, one launch (start us, length us, event | category | flops | bytes accessed | tf_op | source)
XLA Modules:
  0.0 75.6 jit_solution(957707101844083021)
XLA Ops:
  0.6 72.7 %moe_layer.1 = (bf16[96,128]{1,0:T(8,128)(2,1)S(1)}, bf16[96,128]{1,0:T(8,128)(2,1)S(1)}, f32[2,128]{1,0:T(2,128)S(1)}, bf16[3072,256]{1,0:T(8,128)(2,1)S(1)}, b...) custom-call(bf16[128,3072]{1,0:T(8,128)(2,1)} %tok_hbm.1, s32[2,128]{1,0:T(2,128)} %bitcast.14, ...), custom_call_target="tpu_custom_call" | custom-call | tf_op jit(solution)/shard_map/moe_layer/pallas_call | solution.py:408
  73.4 2.3 %settle.1 = (bf16[96,128]{1,0:T(8,128)(2,1)}, bf16[96,128]{1,0:T(8,128)(2,1)}, f32[2,128]{1,0:T(2,128)}, bf16[3072,256]{1,0:T(8,128)(2,1)}, bf16[3072,256]{1,0:T(8,128)(2,1)}, /*index=5*/bf16[256,3072]{1,0:T(8,128)(2,1)}) custom-call(bf16[96,128]{1,0:T(8,128)(2,1)S(1)} %get-tuple-element.18.refs_0_, bf16[96,128]{1,0:T(8,128)(2,1)S(1)} %get-tuple-element.19.refs_1_, ...), custom_call_target="tpu_custom_call" | custom-call | tf_op jit(solution)/shard_map/settle/pallas_call | solution.py:393

commit v4 on v3

v4 whole, which is shorter than its diff:
```python
import jax
import jax.numpy as jnp
from jax import lax
from jax.experimental import pallas as pl
from jax.experimental.pallas import tpu as pltpu
from jax.sharding import PartitionSpec as P

MESH = pl.DeviceIdType.MESH
F32 = jnp.float32
BF16 = jnp.bfloat16

T = 128
D = 3072
HD = 1536
QD = 768
CAP = 40
BLK = 2 * CAP
SLAB = 48
NE = 8
NZ = 8
W = 256
CH = 384
NP = 4

NS = 3

STEPS = ((0, 0), (2, 1), (2, 0), (0, 1), (1, 1), (3, 1), (1, 0), (3, 0))
HALVES = ((0, 1, 2, 3), (4, 5, 6, 7))
HR = 4 * CAP


def nn(a, b):
    return lax.dot_general(a, b, (((1,), (0,)), ((), ())), preferred_element_type=F32)


def nt(a, b):
    return lax.dot_general(a, b, (((1,), (1,)), ((), ())), preferred_element_type=F32)


def tn(a, b):
    return lax.dot_general(a, b, (((0,), (0,)), ((), ())), preferred_element_type=F32)


def iota(shape, axis):
    return lax.broadcasted_iota(jnp.int32, shape, axis)


def kernel(
    tok_hbm, ids_ref, comb_ref, cot_hbm, wg_hbm, wu_hbm, wd_hbm,
    mixed_ref, gtok_ref, gcomb_ref, og, ou, od,
    tc, wg, wu, wd, wgx, wux, wdx, slt, cwt, sendb, rows, acts, actx,
    gsend, grecv, tmat, psend, precv, rsend, rrecv, zsend, zrecv, gzrecv, ysend, yrecv, gycs,
    fsend, frecv,
    lsem, ws_s, ws_r, d_s, d_r, n_s, n_r, c_s, c_r, x_s, x_r, g_s, g_r, q_s, q_r, r_s, r_r,
    z_s, z_r, gz_s, gz_r, y_s, y_r, p_s, p_r,
):
    d = lax.axis_index("dp")
    e = lax.axis_index("expert")
    z, h, c = d // 4, (d // 2) % 2, d % 2
    yl, x = e // 4, e % 4
    twin = (z * 4 + h * 2 + (1 - c), e)
    over = (z * 4 + (1 - h) * 2 + c, e)

    goal = [((yl + dy) % 2) * 4 + (x + dx) % 4 for dx, dy in STEPS]
    origin = [((yl + dy) % 2) * 4 + (x + 4 - dx) % 4 for dx, dy in STEPS]

    def at_z(k):
        return (z + k) % NZ

    def zdev(zz):
        return (zz * 4 + h * 2 + c, e)

    def remote(src, dst, ssem, rsem, dev):
        return pltpu.make_async_remote_copy(
            src_ref=src, dst_ref=dst, send_sem=ssem, recv_sem=rsem, device_id=dev, device_id_type=MESH
        )

    par = z % 2
    quarter = pl.multiple_of(c * HD + par * QD, QD)
    mine = par == c
    last_to, last_from = at_z(5 + 2 * par), at_z(1 + 2 * par)
    last_to_over = (last_to * 4 + (1 - h) * 2 + c, e)
    last_from_over = (last_from * 4 + (1 - h) * 2 + c, e)
    near = (zdev(z + 1 - 2 * par), zdev((z + 2 * par + NZ - 1) % NZ))

    loads = [
        pltpu.make_async_copy(tok_hbm.at[:, pl.ds(quarter, QD)], tc.at[pl.ds(0, T)], lsem.at[0]),
        pltpu.make_async_copy(cot_hbm.at[:, pl.ds(quarter, QD)], tc.at[pl.ds(T, T)], lsem.at[1]),
        pltpu.make_async_copy(wg_hbm, wg, lsem.at[2]),
        pltpu.make_async_copy(wu_hbm, wu, lsem.at[3]),
        pltpu.make_async_copy(wd_hbm, wd, lsem.at[4]),
    ]
    for cp in loads:
        cp.start()

    barrier = pltpu.get_barrier_semaphore()
    for r in range(1, NE):
        pl.semaphore_signal(barrier, inc=1, device_id=(d, goal[r]), device_id_type=MESH)
    for k in range(1, NZ):
        pl.semaphore_signal(barrier, inc=1, device_id=zdev(at_z(k)), device_id_type=MESH)
    pl.semaphore_signal(barrier, inc=1, device_id=twin, device_id_type=MESH)
    pl.semaphore_signal(barrier, inc=1, device_id=over, device_id_type=MESH)
    pl.semaphore_signal(barrier, inc=1, device_id=last_to_over, device_id_type=MESH)
    pl.semaphore_signal(barrier, inc=1, device_id=last_from_over, device_id_type=MESH)

    deep = iota((T, T), 0)
    lane = iota((T, T), 1)
    ids = ids_ref[...]
    comb = comb_ref[...]
    pick0 = deep == ids[0:1]
    pick1 = deep == ids[1:2]
    chosen = jnp.logical_or(pick0, pick1)
    earlier = (deep < lane).astype(F32).astype(BF16)
    rank = nn(chosen.astype(F32).astype(BF16), earlier)
    slot = jnp.where(chosen, rank, -128.0)
    weight = jnp.where(pick0, comb[0:1], 0.0) + jnp.where(pick1, comb[1:2], 0.0)
    slt[...] = jnp.concatenate([slot[0:NE], slot[0:NE]], axis=1)
    cwt[...] = jnp.concatenate([jnp.ones((NE, T), F32), weight[0:NE]], axis=1)

    loads[0].wait()
    loads[1].wait()

    def pack(r):
        j = goal[r]
        slots = slt[pl.ds(j, 1), :]
        weights = cwt[pl.ds(j, 1), :]
        row = iota((BLK, 2 * T), 0)
        col = iota((BLK, 2 * T), 1)
        want = jnp.where(col < T, row, row - CAP).astype(F32)
        hit = want == slots
        scale = jnp.sum(jnp.where(hit, weights, 0.0), axis=1, keepdims=True)
        block = nn(hit.astype(F32).astype(BF16), tc[...])
        sendb[r] = (block * scale).astype(BF16)

    sends = []

    def go(cp):
        cp.start()
        sends.append(cp)

    def spread(r, src):
        for n in range(2):
            part = pl.ds(n * CH, CH)
            go(remote(src.at[:, part], rows.at[c, par, r, :, part], n_s.at[n, r], n_r.at[n, r], near[n]))
        go(remote(src, rows.at[c, par, r], c_s.at[0, r], c_r.at[0, r], twin))

    blocks_out = {r: remote(sendb.at[r], rows.at[c, par, r], d_s.at[r], d_r.at[r], (d, goal[r])) for r in range(1, NE)}
    for r in (1, 2, 3, 0, 4, 5, 6, 7):
        pack(r)
        if r == 1:
            pl.semaphore_wait(barrier, NE - 1 + NZ - 1 + 4)
        if r == 0:
            spread(0, sendb.at[0])
            own = pltpu.make_async_copy(sendb.at[0], rows.at[c, par, 0], lsem.at[5])
            own.start()
        elif r < 4:
            blocks_out[r].start()
    for r in (1, 2, 3):
        blocks_out[r].wait_send()
    for r in HALVES[1]:
        go(blocks_out[r])

    for m in range(NP):
        for n, (src, dst) in enumerate((
            (wd_hbm.at[:, pl.ds(pl.multiple_of((2 * m + 1 - c) * CH, CH), CH)], wdx.at[m]),
            (wg_hbm.at[pl.ds(pl.multiple_of((2 * m + c) * CH, CH), CH)], wgx.at[m]),
            (wu_hbm.at[pl.ds(pl.multiple_of((2 * m + c) * CH, CH), CH)], wux.at[m]),
        )):
            go(remote(src, dst, ws_s.at[n, m], ws_r.at[n, m], twin))

    def expert_of(at):
        return sum(jnp.where(at == r, goal[r], 0) for r in range(NE))

    column = iota((1, NE * BLK), 1)
    expand = (iota((T, NE * BLK), 0) == expert_of(column // BLK)).astype(F32).astype(BF16)
    weight_t = weight.T
    w_hi = weight_t.astype(BF16)
    w_lo = (weight_t - w_hi.astype(F32)).astype(BF16)
    inner = (column % BLK).astype(F32)
    slots_all = nn(slot.T.astype(BF16), expand)
    out_hit = slots_all == inner
    tmat[0:T] = jnp.where(out_hit, nn(w_hi, expand), 0.0).astype(BF16)
    tmat[T:2 * T] = jnp.where(out_hit, nn(w_lo, expand), 0.0).astype(BF16)
    tmat[2 * T:3 * T] = (slots_all == inner - CAP).astype(F32).astype(BF16)

    def pass_on(half):
        for r in HALVES[half]:
            if r:
                here = rows.at[c, par, r]
                remote(here, here, d_s.at[r], d_r.at[r], (d, goal[r])).wait_recv()
                spread(r, here)

    def pass_over(half):
        for r in HALVES[half]:
            there = rows.at[c, 1 - par, r]
            for n in range(2):
                part = there.at[:, pl.ds(n * CH, CH)]
                remote(part, part, n_s.at[n, r], n_r.at[n, r], near[n]).wait_recv()
            go(remote(there, there, c_s.at[1, r], c_r.at[1, r], twin))

    def from_twin(half, n):
        for r in HALVES[half]:
            there = rows.at[1 - c, (1 - par) if n else par, r]
            remote(there, there, c_s.at[n, r], c_r.at[n, r], twin).wait_recv()

    def x_rows(cc, pp, at=pl.ds(0, NE)):
        a = rows[cc, pp, at, 0:SLAB, :]
        return a.reshape(a.shape[0] * SLAB, QD)

    def e_rows(cc, pp, at=pl.ds(0, NE)):
        a = rows[cc, pp, at, BLK - SLAB:BLK, :]
        return a.reshape(a.shape[0] * SLAB, QD)

    def products(half, cc, pp, before=None):
        at = pl.ds(pl.multiple_of(cc * HD + pp * QD, QD), QD)
        blocks = pl.ds(half * 4, 4)
        xs = x_rows(cc, pp, blocks)
        new = nn(xs, wg[at, :]), nn(xs, wu[at, :]), nt(e_rows(cc, pp, blocks), wd[:, at])
        return new if before is None else tuple(u + v for u, v in zip(before, new))

    def first(a):
        return a.reshape(4, SLAB, W)[:, 0:CAP].reshape(HR, W)

    def last(a):
        return a.reshape(4, SLAB, W)[:, SLAB - CAP:].reshape(HR, W)

    swaps = []

    def activate(half, sum3):
        gate, up, hgrad = first(sum3[0]), first(sum3[1]), last(sum3[2])
        sig = jax.nn.sigmoid(gate)
        active = gate * sig
        hidden = (active * up).astype(BF16)
        mine_rows = pl.ds(half * HR, HR)
        acts[0, mine_rows] = hidden
        acts[1, mine_rows] = (hgrad * up * sig * (1.0 + gate * (1.0 - sig))).astype(BF16)
        acts[2, mine_rows] = (hgrad * active).astype(BF16)
        cp = remote(acts.at[:, mine_rows], actx.at[:, mine_rows], x_s.at[half], x_r.at[half], twin)
        go(cp)
        swaps.append(cp)
        dots = jnp.sum(hidden.astype(F32) * hgrad, axis=1, keepdims=True)
        gsend[half * 4:half * 4 + 4] = jnp.broadcast_to(dots, (HR, T)).reshape(4, CAP, T)
        for r in HALVES[half]:
            if r:
                go(remote(gsend.at[r], grecv.at[r], g_s.at[r], g_r.at[r], (d, origin[r])))
            else:
                grecv[0] = gsend[0]

    def by_parity(even, odd):
        return jnp.where(mine, even, odd), jnp.where(mine, odd, even)

    with_0 = at_z(6 - par)
    with_1 = at_z(2 + par)
    pairs_0 = ((with_0 + c) % NZ, (with_0 + 1 - c) % NZ)
    pairs_1 = ((with_1 + NZ - c) % NZ, (with_1 + NZ - 1 + c) % NZ)
    keep = jnp.where(par == 0, pairs_0[0], pairs_1[0]), jnp.where(par == 0, pairs_1[1], pairs_0[1])
    hand = jnp.where(par == 0, pairs_1[0], pairs_0[0]), jnp.where(par == 0, pairs_0[1], pairs_1[1])
    targets = (by_parity(at_z(4), at_z(3 - 2 * par)), keep, by_parity(z, last_to))

    def own_sums(half, to):
        at = pl.ds(half * HR, HR)
        oc = pl.multiple_of(to[0] * CH, CH)
        tcol = pl.multiple_of(to[1] * CH, CH)
        out = nn(acts[0, at], wd[:, pl.ds(oc, CH)])
        return out, nt(acts[1, at], wg[pl.ds(tcol, CH), :]) + nt(acts[2, at], wu[pl.ds(tcol, CH), :])

    def chip_sums(half, to, own_part=None):
        at = pl.ds(half * HR, HR)
        out, back = own_sums(half, to) if own_part is None else own_part
        out = out + nn(actx[0, at], wdx[to[0] // 2])
        return out, back + nt(actx[1, at], wgx[to[1] // 2]) + nt(actx[2, at], wux[to[1] // 2])

    def pair_copies(half):
        at = pl.ds(half * HR, HR)
        z_0, z_1 = z + 1 - 2 * par, (z + 2 * par + NZ - 1) % NZ
        to = zdev(jnp.where(par == 0, z_1, z_0)), zdev(jnp.where(par == 0, z_0, z_1))
        return [
            remote(psend.at[n, at], precv.at[n, at], q_s.at[half, n], q_r.at[half, n], to[n]) for n in range(2)
        ]

    def hand_over(half, own_part):
        at = pl.ds(half * HR, HR)
        sums = chip_sums(half, hand, own_part)
        for n in range(2):
            psend[n, at] = sums[n].astype(BF16)
        for cp in pair_copies(half):
            go(cp)

    given = []

    def give_back(half, s):
        out, back = chip_sums(half, targets[s])
        if s == 1:
            at = pl.ds(half * HR, HR)
            for cp in pair_copies(half):
                cp.wait_recv()
            out, back = out + precv[0, at].astype(F32), back + precv[1, at].astype(F32)
        both = jnp.concatenate([out.reshape(4, CAP, CH), back.reshape(4, CAP, CH)], axis=1)
        rsend[s, half * 4:half * 4 + 4] = both.astype(BF16)
        copies = [
            remote(rsend.at[s, r], rrecv.at[s, r], r_s.at[s, r], r_r.at[s, r], (d, origin[r]))
            for r in HALVES[half] if r
        ]
        if half == 0:
            rrecv[s, 0] = rsend[s, 0]
        if len(given) >= 2:
            for cp in given[-2]:
                cp.wait_send()
        for cp in copies:
            cp.start()
        given.append(copies)

    pass_on(0)
    own.wait()
    for cp in loads[2:]:
        cp.wait()
    sum_a = products(0, c, par)
    from_twin(0, 0)
    sum_a = products(0, 1 - c, par, sum_a)
    pass_on(1)
    sum_b = products(1, c, par)
    pass_over(0)
    sum_a = products(0, c, 1 - par, sum_a)
    from_twin(0, 1)
    sum_a = products(0, 1 - c, 1 - par, sum_a)
    activate(0, sum_a)
    from_twin(1, 0)
    sum_b = products(1, 1 - c, par, sum_b)
    start = own_sums(0, hand)
    for n in range(3):
        for m in range(NP):
            there = (wdx, wgx, wux)[n].at[m]
            remote(there, there, ws_s.at[n, m], ws_r.at[n, m], twin).wait_recv()
    swaps[0].wait_recv()
    hand_over(0, start)
    give_back(0, 0)
    give_back(0, 2)
    pass_over(1)
    sum_b = products(1, c, 1 - par, sum_b)
    from_twin(1, 1)
    sum_b = products(1, 1 - c, 1 - par, sum_b)
    activate(1, sum_b)
    start = own_sums(1, hand)
    swaps[1].wait_recv()
    hand_over(1, start)
    give_back(1, 0)
    give_back(0, 1)
    give_back(1, 1)

    for r in range(1, NE):
        remote(gsend.at[r], grecv.at[r], g_s.at[r], g_r.at[r], (d, goal[r])).wait_recv()
    q = iota((NE * CAP, T), 0).astype(F32)
    values = grecv[...].reshape(NE * CAP, T)

    slot_of = sum(jnp.where(deep == goal[r], r, 0) for r in range(1, NE)).astype(F32) * CAP + rank

    def gathered(pick, c_row):
        place = jnp.sum(jnp.where(pick, slot_of, 0.0), axis=0, keepdims=True)
        return jnp.sum(jnp.where(q == place, values, 0.0), axis=0, keepdims=True) / c_row

    sub = iota((8, T), 0)
    gzrecv[z] = jnp.where(
        sub == 0, gathered(pick0, comb[0:1]), jnp.where(sub == 1, gathered(pick1, comb[1:2]), 0.0)
    )
    for k in range(1, NZ):
        go(remote(gzrecv.at[z], gzrecv.at[z], gz_s.at[k], gz_r.at[z], zdev(at_z(k))))

    def padded(a, lead):
        a = a.astype(F32).reshape(NE, CAP, W)
        zero = jnp.zeros((NE, SLAB - CAP, W), F32)
        a = jnp.concatenate([a, zero] if lead else [zero, a], axis=1)
        return a.reshape(NE * SLAB, W).astype(BF16)

    hid_pad = padded(acts[0], False)
    pair_pad = jnp.concatenate([padded(acts[1], True), padded(acts[2], True)], axis=1)
    def weight_grads(k):
        at = k * QD
        both = tn(x_rows(k // 2, k % 2), pair_pad)
        og[at:at + QD] = both[:, 0:W].astype(BF16)
        ou[at:at + QD] = both[:, W:2 * W].astype(BF16)
        od[:, at:at + QD] = tn(hid_pad, e_rows(k // 2, k % 2)).astype(BF16)

    windows = [pl.ds(pl.multiple_of(T * hh, T), 2 * T) for hh in (h, 1 - h)]
    def to_tokens(s):
        for r in range(1, NE):
            remote(rsend.at[s, r], rrecv.at[s, r], r_s.at[s, r], r_r.at[s, r], (d, goal[r])).wait_recv()
        sums = nn(tmat[...], rrecv[s].reshape(NE * BLK, CH))
        mix = sums[0:T] + sums[T:2 * T]
        back = sums[2 * T:3 * T]
        if s < NS - 1:
            zsend[s, 0] = mix.astype(BF16)
            zsend[s, 1] = back.astype(BF16)
            for n in range(2):
                go(remote(zsend.at[s, n], zrecv.at[z], z_s.at[s, n], z_r.at[z], zdev(targets[s][n])))
        else:
            zsend[s, 0] = jnp.where(mine, back, mix).astype(BF16)
            for n, (src, dev) in enumerate((
                (zsend.at[s, 0, :, windows[0]], zdev(last_to)),
                (zsend.at[s, 0, :, windows[1]], last_to_over),
            )):
                go(remote(src, yrecv.at[n], y_s.at[n], y_r.at[n], dev))
            return jnp.where(mine, mix, back)

    give_back(1, 2)
    weight_grads(0)
    to_tokens(0)
    weight_grads(1)
    to_tokens(1)
    weight_grads(2)
    for k in range(1, NZ):
        zz = at_z(k)
        remote(gzrecv.at[zz], gzrecv.at[zz], gz_s.at[k], gz_r.at[zz], zdev(zz)).wait_recv()
    gc_sum = gzrecv[0]
    for k in range(1, NZ):
        gc_sum = gc_sum + gzrecv[k]
    gycs[0] = gc_sum
    gy = remote(gycs.at[0], gycs.at[1], p_s.at[0], p_r.at[0], over)
    gy.start()
    weight_grads(3)
    gy.wait_recv()
    gc_sum = gc_sum + gycs[1]
    gycs[2] = gc_sum
    gx = remote(gycs.at[2], gycs.at[3], p_s.at[1], p_r.at[1], twin)
    gx.start()
    total = to_tokens(NS - 1)
    steps = (
        4, jnp.where(par == 0, 1, 3),
        jnp.where(mine, 6 + par, 2 - par), jnp.where(mine, 3 - par, 5 + par),
    )
    for k in steps:
        zz = at_z(NZ - k)
        remote(zsend.at[0, 0], zrecv.at[zz], z_s.at[0, 0], z_r.at[zz], zdev(zz)).wait_recv()
        total = total + zrecv[zz].astype(F32)
    ysend[...] = total.astype(BF16)
    yc = remote(ysend.at[:, windows[1]], yrecv.at[2], y_s.at[2], y_r.at[2], over)
    yc.start()
    for n in range(3):
        remote(yrecv.at[n], yrecv.at[n], y_s.at[n], y_r.at[n], over).wait_recv()
    window = jnp.where(h == 0, total[:, 0:2 * T], total[:, T:3 * T])
    window = window + yrecv[0].astype(F32) + yrecv[1].astype(F32) + yrecv[2].astype(F32)
    final = window.astype(BF16)
    fsend[...] = final
    fc = remote(fsend, frecv, p_s.at[2], p_r.at[2], twin)
    fc.start()
    shift = 64 * h + 96 * c
    pick = (iota((T, 2 * T), 1) == iota((T, 2 * T), 0) + shift).astype(F32).astype(BF16)
    gx.wait_recv()
    gc_sum = gc_sum + gycs[3]
    gcomb_ref[...] = gc_sum[0:2]
    a = nt(pick, final)
    fc.wait_recv()
    b = nt(pick, frecv[...])
    mixed_ref[...] = jnp.where(mine, a, b)[0:96].astype(BF16)
    gtok_ref[...] = jnp.where(mine, b, a)[0:96].astype(BF16)

    for cp in sends + given[-2] + given[-1]:
        cp.wait_send()
    for cp in (gy, yc, gx, fc):
        cp.wait_send()


def settle_kernel(*refs):
    copies = [pltpu.make_async_copy(refs[i], refs[6 + i], refs[12].at[i]) for i in range(6)]
    for cp in copies:
        cp.start()
    for cp in copies:
        cp.wait()


def settle(*arrays):
    any_spec = pl.BlockSpec(memory_space=pl.ANY)
    return pl.pallas_call(
        settle_kernel,
        out_shape=tuple(jax.ShapeDtypeStruct(a.shape, a.dtype) for a in arrays),
        in_specs=[any_spec] * 6,
        out_specs=(any_spec,) * 6,
        scratch_shapes=[pltpu.SemaphoreType.DMA((6,))],
        compiler_params=pltpu.CompilerParams(vmem_limit_bytes=16 * 1024 * 1024),
        name="settle",
    )(*arrays)


def local(tokens, expert_ids, combine, cotangent, w_gate, w_up, w_down):
    any_spec = pl.BlockSpec(memory_space=pl.ANY)
    vmem = pl.BlockSpec(memory_space=pltpu.VMEM)
    dma = pltpu.SemaphoreType.DMA
    mixed, gtok, gcomb, gg, gu, gd = pl.pallas_call(
        kernel,
        out_shape=(
            pltpu.VMEM((96, T), BF16),
            pltpu.VMEM((96, T), BF16),
            pltpu.VMEM((2, T), F32),
            pltpu.VMEM((D, W), BF16),
            pltpu.VMEM((D, W), BF16),
            pltpu.VMEM((W, D), BF16),
        ),
        in_specs=[any_spec, vmem, vmem, any_spec, any_spec, any_spec, any_spec],
        out_specs=(vmem,) * 6,
        scratch_shapes=[
            pltpu.VMEM((2 * T, QD), BF16),
            pltpu.VMEM((D, W), BF16),
            pltpu.VMEM((D, W), BF16),
            pltpu.VMEM((W, D), BF16),
            pltpu.VMEM((NP, CH, W), BF16),
            pltpu.VMEM((NP, CH, W), BF16),
            pltpu.VMEM((NP, W, CH), BF16),
            pltpu.VMEM((NE, 2 * T), F32),
            pltpu.VMEM((NE, 2 * T), F32),
            pltpu.VMEM((NE, BLK, QD), BF16),
            pltpu.VMEM((2, 2, NE, BLK, QD), BF16),
            pltpu.VMEM((3, NE * CAP, W), BF16),
            pltpu.VMEM((3, NE * CAP, W), BF16),
            pltpu.VMEM((NE, CAP, T), F32),
            pltpu.VMEM((NE, CAP, T), F32),
            pltpu.VMEM((3 * T, NE * BLK), BF16),
            pltpu.VMEM((2, NE * CAP, CH), BF16),
            pltpu.VMEM((2, NE * CAP, CH), BF16),
            pltpu.VMEM((NS, NE, BLK, CH), BF16),
            pltpu.VMEM((NS, NE, BLK, CH), BF16),
            pltpu.VMEM((NS, 2, T, CH), BF16),
            pltpu.VMEM((NZ, T, CH), BF16),
            pltpu.VMEM((NZ, 8, T), F32),
            pltpu.VMEM((T, CH), BF16),
            pltpu.VMEM((3, T, 2 * T), BF16),
            pltpu.VMEM((4, 8, T), F32),
            pltpu.VMEM((T, 2 * T), BF16),
            pltpu.VMEM((T, 2 * T), BF16),
            dma((6,)),
            dma((3, NP)),
            dma((3, NP)),
            dma((NE,)),
            dma((NE,)),
            dma((2, 8)),
            dma((2, NE)),
            dma((2, 8)),
            dma((2, NE)),
            dma((2,)),
            dma((2,)),
            dma((NE,)),
            dma((NE,)),
            dma((2, 2)),
            dma((2, 2)),
            dma((NS, NE)),
            dma((NS, NE)),
            dma((NS, 2)),
            dma((NZ,)),
            dma((NZ,)),
            dma((NZ,)),
            dma((3,)),
            dma((3,)),
            dma((3,)),
            dma((3,)),
        ],
        compiler_params=pltpu.CompilerParams(
            collective_id=0, has_side_effects=True, vmem_limit_bytes=59 * 1024 * 1024
        ),
        name="moe_layer",
    )(tokens, expert_ids.T, combine.T, cotangent, w_gate[0], w_up[0], w_down[0])
    mixed, gtok, gcomb, gg, gu, gd = settle(mixed, gtok, gcomb, gg, gu, gd)
    return mixed.T, gtok.T, gcomb.T, gg[None], gu[None], gd[None]


def solution(mesh):
    in_specs = (
        P("expert", None),
        P("expert", None),
        P("expert", None),
        P("expert", None),
        P("expert", None, "dp"),
        P("expert", None, "dp"),
        P("expert", "dp", None),
    )
    out_specs = (
        P("expert", "dp"),
        P("expert", "dp"),
        P("expert", None),
        P("expert", None, "dp"),
        P("expert", None, "dp"),
        P("expert", "dp", None),
    )
    return jax.shard_map(local, mesh=mesh, in_specs=in_specs, out_specs=out_specs, check_vma=False)
```

time: 75.9 us -> 71.4 us (0.941)
  Pallas kernels: 75 us -> 70.7 us
    pallas_call x1, Pallas kernels: 72.7 us -> 68.4 us  [local(): pl.pallas_call(kernel, out_shape=(pltpu.VMEM((96, T), BF16), pltpu.VMEM((...]
where the time goes in v4:
time: 71.4 us; the launch traced here: 71.3 us
  Pallas kernels  70.7 us (99%)
    pallas_call x1, Pallas kernels, local(): pl.pallas_call(kernel, out_shape=(pltpu.VMEM((96, T), BF16), pltpu.VMEM((...  68.4 us
    pallas_call x1, Pallas kernels, settle(): pl.pallas_call(settle_kernel, out_shape=tuple((jax.ShapeDtypeStruct(a.sha...  2.25 us

profile of v4, /device:TPU:1, one launch (start us, length us, event | category | flops | bytes accessed | tf_op | source)
XLA Modules:
  0.0 71.3 jit_solution(16167383291651539183)
XLA Ops:
  0.6 68.4 %moe_layer.1 = (bf16[96,128]{1,0:T(8,128)(2,1)S(1)}, bf16[96,128]{1,0:T(8,128)(2,1)S(1)}, f32[2,128]{1,0:T(2,128)S(1)}, bf16[3072,256]{1,0:T(8,128)(2,1)S(1)}, b...) custom-call(bf16[128,3072]{1,0:T(8,128)(2,1)} %tok_hbm.1, s32[2,128]{1,0:T(2,128)} %bitcast.14, ...), custom_call_target="tpu_custom_call" | custom-call | tf_op jit(solution)/shard_map/moe_layer/pallas_call | solution.py:487
  69.1 2.3 %settle.1 = (bf16[96,128]{1,0:T(8,128)(2,1)}, bf16[96,128]{1,0:T(8,128)(2,1)}, f32[2,128]{1,0:T(2,128)}, bf16[3072,256]{1,0:T(8,128)(2,1)}, bf16[3072,256]{1,0:T(8,128)(2,1)}, /*index=5*/bf16[256,3072]{1,0:T(8,128)(2,1)}) custom-call(bf16[96,128]{1,0:T(8,128)(2,1)S(1)} %get-tuple-element.18.refs_0_, bf16[96,128]{1,0:T(8,128)(2,1)S(1)} %get-tuple-element.19.refs_1_, ...), custom_call_target="tpu_custom_call" | custom-call | tf_op jit(solution)/shard_map/settle/pallas_call | solution.py:472

commit v5 on v4

--- a/solution.py
+++ b/solution.py
@@ -26,6 +26,7 @@
 
 STEPS = ((0, 0), (2, 1), (2, 0), (0, 1), (1, 1), (3, 1), (1, 0), (3, 0))
 HALVES = ((0, 1, 2, 3), (4, 5, 6, 7))
+WHOLE = (0, 6, 7)
 HR = 4 * CAP
 
 
@@ -48,11 +49,11 @@
 def kernel(
     tok_hbm, ids_ref, comb_ref, cot_hbm, wg_hbm, wu_hbm, wd_hbm,
     mixed_ref, gtok_ref, gcomb_ref, og, ou, od,
-    tc, wg, wu, wd, wgx, wux, wdx, slt, cwt, sendb, rows, acts, actx,
+    tc, tc_2, wg, wu, wd, wgx, wux, wdx, slt, cwt, sendb, sendx, rows, acts, actx,
     gsend, grecv, tmat, psend, precv, rsend, rrecv, zsend, zrecv, gzrecv, ysend, yrecv, gycs,
     fsend, frecv,
-    lsem, ws_s, ws_r, d_s, d_r, n_s, n_r, c_s, c_r, x_s, x_r, g_s, g_r, q_s, q_r, r_s, r_r,
-    z_s, z_r, gz_s, gz_r, y_s, y_r, p_s, p_r,
+    lsem, ws_s, ws_r, d_s, d_r, w_s, w_r, n_s, n_r, c_s, c_r, x_s, x_r, g_s, g_r, q_s, q_r, r_s, r_r,
+    z_s, z_r, gz_s, gz_r, k_s, y_s, y_r, p_s, p_r,
 ):
     d = lax.axis_index("dp")
     e = lax.axis_index("expert")
@@ -77,8 +78,11 @@
 
     par = z % 2
     quarter = pl.multiple_of(c * HD + par * QD, QD)
+    quarter_2 = pl.multiple_of(c * HD + (1 - par) * QD, QD)
     mine = par == c
-    last_to, last_from = at_z(5 + 2 * par), at_z(1 + 2 * par)
+    up, down = 3 - 2 * par, 5 + 2 * par
+    last_to = at_z(jnp.where(c == 0, down, up))
+    last_from = at_z(jnp.where(c == 0, 1 + 2 * par, 7 - 2 * par))
     last_to_over = (last_to * 4 + (1 - h) * 2 + c, e)
     last_from_over = (last_from * 4 + (1 - h) * 2 + c, e)
     near = (zdev(z + 1 - 2 * par), zdev((z + 2 * par + NZ - 1) % NZ))
@@ -86,9 +90,11 @@
     loads = [
         pltpu.make_async_copy(tok_hbm.at[:, pl.ds(quarter, QD)], tc.at[pl.ds(0, T)], lsem.at[0]),
         pltpu.make_async_copy(cot_hbm.at[:, pl.ds(quarter, QD)], tc.at[pl.ds(T, T)], lsem.at[1]),
-        pltpu.make_async_copy(wg_hbm, wg, lsem.at[2]),
-        pltpu.make_async_copy(wu_hbm, wu, lsem.at[3]),
-        pltpu.make_async_copy(wd_hbm, wd, lsem.at[4]),
+        pltpu.make_async_copy(tok_hbm.at[:, pl.ds(quarter_2, QD)], tc_2.at[pl.ds(0, T)], lsem.at[2]),
+        pltpu.make_async_copy(cot_hbm.at[:, pl.ds(quarter_2, QD)], tc_2.at[pl.ds(T, T)], lsem.at[3]),
+        pltpu.make_async_copy(wg_hbm, wg, lsem.at[4]),
+        pltpu.make_async_copy(wu_hbm, wu, lsem.at[5]),
+        pltpu.make_async_copy(wd_hbm, wd, lsem.at[6]),
     ]
     for cp in loads:
         cp.start()
@@ -102,6 +108,9 @@
     pl.semaphore_signal(barrier, inc=1, device_id=over, device_id_type=MESH)
     pl.semaphore_signal(barrier, inc=1, device_id=last_to_over, device_id_type=MESH)
     pl.semaphore_signal(barrier, inc=1, device_id=last_from_over, device_id_type=MESH)
+    for k in (jnp.where(mine, 6 + par, 2 - par), jnp.where(mine, 3 - par, 5 + par)):
+        giver = (at_z(NZ - k) * 4 + (1 - h) * 2 + c, e)
+        pl.semaphore_signal(barrier, inc=1, device_id=giver, device_id_type=MESH)
 
     deep = iota((T, T), 0)
     lane = iota((T, T), 1)
@@ -120,7 +129,7 @@
     loads[0].wait()
     loads[1].wait()
 
-    def pack(r):
+    def pack(r, source, to):
         j = goal[r]
         slots = slt[pl.ds(j, 1), :]
         weights = cwt[pl.ds(j, 1), :]
@@ -129,8 +138,8 @@
         want = jnp.where(col < T, row, row - CAP).astype(F32)
         hit = want == slots
         scale = jnp.sum(jnp.where(hit, weights, 0.0), axis=1, keepdims=True)
-        block = nn(hit.astype(F32).astype(BF16), tc[...])
-        sendb[r] = (block * scale).astype(BF16)
+        block = nn(hit.astype(F32).astype(BF16), source[...])
+        to[...] = (block * scale).astype(BF16)
 
     sends = []
 
@@ -139,26 +148,29 @@
         sends.append(cp)
 
     def spread(r, src):
-        for n in range(2):
+        for n in range(2 if r not in WHOLE else 0):
             part = pl.ds(n * CH, CH)
             go(remote(src.at[:, part], rows.at[c, par, r, :, part], n_s.at[n, r], n_r.at[n, r], near[n]))
         go(remote(src, rows.at[c, par, r], c_s.at[0, r], c_r.at[0, r], twin))
 
     blocks_out = {r: remote(sendb.at[r], rows.at[c, par, r], d_s.at[r], d_r.at[r], (d, goal[r])) for r in range(1, NE)}
     for r in (1, 2, 3, 0, 4, 5, 6, 7):
-        pack(r)
+        pack(r, tc, sendb.at[r] if r else rows.at[c, par, 0])
         if r == 1:
-            pl.semaphore_wait(barrier, NE - 1 + NZ - 1 + 4)
+            pl.semaphore_wait(barrier, NE - 1 + NZ - 1 + 6)
         if r == 0:
-            spread(0, sendb.at[0])
-            own = pltpu.make_async_copy(sendb.at[0], rows.at[c, par, 0], lsem.at[5])
-            own.start()
+            spread(0, rows.at[c, par, 0])
         elif r < 4:
             blocks_out[r].start()
     for r in (1, 2, 3):
         blocks_out[r].wait_send()
     for r in HALVES[1]:
-        go(blocks_out[r])
+        blocks_out[r].start()
+    loads[2].wait()
+    loads[3].wait()
+    for n, r in enumerate(WHOLE):
+        pack(r, tc_2, sendx.at[n] if r else rows.at[c, 1 - par, 0])
+    go(remote(rows.at[c, 1 - par, 0], rows.at[c, 1 - par, 0], c_s.at[1, 0], c_r.at[1, 0], twin))
 
     for m in range(NP):
         for n, (src, dst) in enumerate((
@@ -192,8 +204,12 @@
 
     def pass_over(half):
         for r in HALVES[half]:
+            if r == 0:
+                continue
             there = rows.at[c, 1 - par, r]
-            for n in range(2):
+            if r in WHOLE:
+                remote(there, there, w_s.at[r], w_r.at[r], (d, goal[r])).wait_recv()
+            for n in range(2 if r not in WHOLE else 0):
                 part = there.at[:, pl.ds(n * CH, CH)]
                 remote(part, part, n_s.at[n, r], n_r.at[n, r], near[n]).wait_recv()
             go(remote(there, there, c_s.at[1, r], c_r.at[1, r], twin))
@@ -255,7 +271,7 @@
     pairs_1 = ((with_1 + NZ - c) % NZ, (with_1 + NZ - 1 + c) % NZ)
     keep = jnp.where(par == 0, pairs_0[0], pairs_1[0]), jnp.where(par == 0, pairs_1[1], pairs_0[1])
     hand = jnp.where(par == 0, pairs_1[0], pairs_0[0]), jnp.where(par == 0, pairs_0[1], pairs_1[1])
-    targets = (by_parity(at_z(4), at_z(3 - 2 * par)), keep, by_parity(z, last_to))
+    targets = (by_parity(at_z(4), at_z(jnp.where(c == 0, up, down))), keep, by_parity(z, last_to))
 
     def own_sums(half, to):
         at = pl.ds(half * HR, HR)
@@ -285,8 +301,6 @@
             psend[n, at] = sums[n].astype(BF16)
         for cp in pair_copies(half):
             go(cp)
-
-    given = []
 
     def give_back(half, s):
         out, back = chip_sums(half, targets[s])
@@ -303,16 +317,16 @@
         ]
         if half == 0:
             rrecv[s, 0] = rsend[s, 0]
-        if len(given) >= 2:
-            for cp in given[-2]:
-                cp.wait_send()
         for cp in copies:
-            cp.start()
-        given.append(copies)
+            go(cp)
 
     pass_on(0)
-    own.wait()
-    for cp in loads[2:]:
+    for r in HALVES[1]:
+        blocks_out[r].wait_send()
+    for n, r in enumerate(WHOLE):
+        if r:
+            go(remote(sendx.at[n], rows.at[c, 1 - par, r], w_s.at[r], w_r.at[r], (d, goal[r])))
+    for cp in loads[4:]:
         cp.wait()
     sum_a = products(0, c, par)
     from_twin(0, 0)
@@ -391,6 +405,13 @@
             zsend[s, 0] = mix.astype(BF16)
             zsend[s, 1] = back.astype(BF16)
             for n in range(2):
+                if s == 1:
+                    for w in range(2):
+                        slot = 3 + 2 * par + w
+                        dev = (targets[s][n] * 4 + (h + w) % 2 * 2 + c, e)
+                        part = zsend.at[s, n, :, windows[w]]
+                        go(remote(part, yrecv.at[slot], k_s.at[n, w], y_r.at[slot], dev))
+                    continue
                 go(remote(zsend.at[s, n], zrecv.at[z], z_s.at[s, n], z_r.at[z], zdev(targets[s][n])))
         else:
             zsend[s, 0] = jnp.where(mine, back, mix).astype(BF16)
@@ -407,6 +428,8 @@
     weight_grads(1)
     to_tokens(1)
     weight_grads(2)
+    weight_grads(3)
+    total = to_tokens(NS - 1)
     for k in range(1, NZ):
         zz = at_z(k)
         remote(gzrecv.at[zz], gzrecv.at[zz], gz_s.at[k], gz_r.at[zz], zdev(zz)).wait_recv()
@@ -416,28 +439,23 @@
     gycs[0] = gc_sum
     gy = remote(gycs.at[0], gycs.at[1], p_s.at[0], p_r.at[0], over)
     gy.start()
-    weight_grads(3)
-    gy.wait_recv()
-    gc_sum = gc_sum + gycs[1]
-    gycs[2] = gc_sum
-    gx = remote(gycs.at[2], gycs.at[3], p_s.at[1], p_r.at[1], twin)
-    gx.start()
-    total = to_tokens(NS - 1)
-    steps = (
-        4, jnp.where(par == 0, 1, 3),
-        jnp.where(mine, 6 + par, 2 - par), jnp.where(mine, 3 - par, 5 + par),
-    )
-    for k in steps:
+    for k in (4, jnp.where(c == 0, 1 + 2 * par, 7 - 2 * par)):
         zz = at_z(NZ - k)
         remote(zsend.at[0, 0], zrecv.at[zz], z_s.at[0, 0], z_r.at[zz], zdev(zz)).wait_recv()
         total = total + zrecv[zz].astype(F32)
     ysend[...] = total.astype(BF16)
     yc = remote(ysend.at[:, windows[1]], yrecv.at[2], y_s.at[2], y_r.at[2], over)
     yc.start()
-    for n in range(3):
-        remote(yrecv.at[n], yrecv.at[n], y_s.at[n], y_r.at[n], over).wait_recv()
+    gy.wait_recv()
+    gc_sum = gc_sum + gycs[1]
+    gycs[2] = gc_sum
+    gx = remote(gycs.at[2], gycs.at[3], p_s.at[1], p_r.at[1], twin)
+    gx.start()
+    for n in range(7):
+        remote(yrecv.at[n], yrecv.at[n], y_s.at[0], y_r.at[n], over).wait_recv()
     window = jnp.where(h == 0, total[:, 0:2 * T], total[:, T:3 * T])
-    window = window + yrecv[0].astype(F32) + yrecv[1].astype(F32) + yrecv[2].astype(F32)
+    for n in range(7):
+        window = window + yrecv[n].astype(F32)
     final = window.astype(BF16)
     fsend[...] = final
     fc = remote(fsend, frecv, p_s.at[2], p_r.at[2], twin)
@@ -453,7 +471,7 @@
     mixed_ref[...] = jnp.where(mine, a, b)[0:96].astype(BF16)
     gtok_ref[...] = jnp.where(mine, b, a)[0:96].astype(BF16)
 
-    for cp in sends + given[-2] + given[-1]:
+    for cp in sends:
         cp.wait_send()
     for cp in (gy, yc, gx, fc):
         cp.wait_send()
@@ -498,6 +516,7 @@
         out_specs=(vmem,) * 6,
         scratch_shapes=[
             pltpu.VMEM((2 * T, QD), BF16),
+            pltpu.VMEM((2 * T, QD), BF16),
             pltpu.VMEM((D, W), BF16),
             pltpu.VMEM((D, W), BF16),
             pltpu.VMEM((W, D), BF16),
@@ -507,6 +526,7 @@
             pltpu.VMEM((NE, 2 * T), F32),
             pltpu.VMEM((NE, 2 * T), F32),
             pltpu.VMEM((NE, BLK, QD), BF16),
+            pltpu.VMEM((3, BLK, QD), BF16),
             pltpu.VMEM((2, 2, NE, BLK, QD), BF16),
             pltpu.VMEM((3, NE * CAP, W), BF16),
             pltpu.VMEM((3, NE * CAP, W), BF16),
@@ -521,13 +541,15 @@
             pltpu.VMEM((NZ, T, CH), BF16),
             pltpu.VMEM((NZ, 8, T), F32),
             pltpu.VMEM((T, CH), BF16),
-            pltpu.VMEM((3, T, 2 * T), BF16),
+            pltpu.VMEM((7, T, 2 * T), BF16),
             pltpu.VMEM((4, 8, T), F32),
             pltpu.VMEM((T, 2 * T), BF16),
             pltpu.VMEM((T, 2 * T), BF16),
-            dma((6,)),
+            dma((7,)),
             dma((3, NP)),
             dma((3, NP)),
+            dma((NE,)),
+            dma((NE,)),
             dma((NE,)),
             dma((NE,)),
             dma((2, 8)),
@@ -546,8 +568,9 @@
             dma((NZ,)),
             dma((NZ,)),
             dma((NZ,)),
+            dma((2, 2)),
             dma((3,)),
-            dma((3,)),
+            dma((7,)),
             dma((3,)),
             dma((3,)),
         ],

time: 71.4 us -> 70.2 us (0.983)
  Pallas kernels: 70.7 us -> 69.5 us
    pallas_call x1, Pallas kernels: 68.4 us -> 67.2 us  [local(): pl.pallas_call(kernel, out_shape=(pltpu.VMEM((96, T), BF16), pltpu.VMEM((...]
where the time goes in v5:
time: 70.2 us; the launch traced here: 70.1 us
  Pallas kernels  69.5 us (99%)
    pallas_call x1, Pallas kernels, local(): pl.pallas_call(kernel, out_shape=(pltpu.VMEM((96, T), BF16), pltpu.VMEM((...  67.2 us
    pallas_call x1, Pallas kernels, settle(): pl.pallas_call(settle_kernel, out_shape=tuple((jax.ShapeDtypeStruct(a.sha...  2.25 us

profile of v5, /device:TPU:1, one launch (start us, length us, event | category | flops | bytes accessed | tf_op | source)
XLA Modules:
  0.0 70.1 jit_solution(4903935904605808259)
XLA Ops:
  0.6 67.2 %moe_layer.1 = (bf16[96,128]{1,0:T(8,128)(2,1)S(1)}, bf16[96,128]{1,0:T(8,128)(2,1)S(1)}, f32[2,128]{1,0:T(2,128)S(1)}, bf16[3072,256]{1,0:T(8,128)(2,1)S(1)}, b...) custom-call(bf16[128,3072]{1,0:T(8,128)(2,1)} %tok_hbm.1, s32[2,128]{1,0:T(2,128)} %bitcast.14, ...), custom_call_target="tpu_custom_call" | custom-call | tf_op jit(solution)/shard_map/moe_layer/pallas_call | solution.py:505
  67.9 2.3 %settle.1 = (bf16[96,128]{1,0:T(8,128)(2,1)}, bf16[96,128]{1,0:T(8,128)(2,1)}, f32[2,128]{1,0:T(2,128)}, bf16[3072,256]{1,0:T(8,128)(2,1)}, bf16[3072,256]{1,0:T(8,128)(2,1)}, /*index=5*/bf16[256,3072]{1,0:T(8,128)(2,1)}) custom-call(bf16[96,128]{1,0:T(8,128)(2,1)S(1)} %get-tuple-element.18.refs_0_, bf16[96,128]{1,0:T(8,128)(2,1)S(1)} %get-tuple-element.19.refs_1_, ...), custom_call_target="tpu_custom_call" | custom-call | tf_op jit(solution)/shard_map/settle/pallas_call | solution.py:490

commit v6 on v5

--- a/solution.py
+++ b/solution.py
@@ -80,12 +80,25 @@
     quarter = pl.multiple_of(c * HD + par * QD, QD)
     quarter_2 = pl.multiple_of(c * HD + (1 - par) * QD, QD)
     mine = par == c
-    up, down = 3 - 2 * par, 5 + 2 * par
+    up, down = 1, NZ - 1
     last_to = at_z(jnp.where(c == 0, down, up))
-    last_from = at_z(jnp.where(c == 0, 1 + 2 * par, 7 - 2 * par))
+    last_from = at_z(jnp.where(c == 0, up, down))
     last_to_over = (last_to * 4 + (1 - h) * 2 + c, e)
     last_from_over = (last_from * 4 + (1 - h) * 2 + c, e)
     near = (zdev(z + 1 - 2 * par), zdev((z + 2 * par + NZ - 1) % NZ))
+
+    barrier = pltpu.get_barrier_semaphore()
+    for r in range(1, NE):
+        pl.semaphore_signal(barrier, inc=1, device_id=(d, goal[r]), device_id_type=MESH)
+    for k in range(1, NZ):
+        pl.semaphore_signal(barrier, inc=1, device_id=zdev(at_z(k)), device_id_type=MESH)
+    pl.semaphore_signal(barrier, inc=1, device_id=twin, device_id_type=MESH)
+    pl.semaphore_signal(barrier, inc=1, device_id=over, device_id_type=MESH)
+    pl.semaphore_signal(barrier, inc=1, device_id=last_to_over, device_id_type=MESH)
+    pl.semaphore_signal(barrier, inc=1, device_id=last_from_over, device_id_type=MESH)
+    for k in (jnp.where(mine, 6, 2), jnp.where(mine, 3, 5)):
+        giver = (at_z(NZ - k) * 4 + (1 - h) * 2 + c, e)
+        pl.semaphore_signal(barrier, inc=1, device_id=giver, device_id_type=MESH)
 
     loads = [
         pltpu.make_async_copy(tok_hbm.at[:, pl.ds(quarter, QD)], tc.at[pl.ds(0, T)], lsem.at[0]),
@@ -98,19 +111,6 @@
     ]
     for cp in loads:
         cp.start()
-
-    barrier = pltpu.get_barrier_semaphore()
-    for r in range(1, NE):
-        pl.semaphore_signal(barrier, inc=1, device_id=(d, goal[r]), device_id_type=MESH)
-    for k in range(1, NZ):
-        pl.semaphore_signal(barrier, inc=1, device_id=zdev(at_z(k)), device_id_type=MESH)
-    pl.semaphore_signal(barrier, inc=1, device_id=twin, device_id_type=MESH)
-    pl.semaphore_signal(barrier, inc=1, device_id=over, device_id_type=MESH)
-    pl.semaphore_signal(barrier, inc=1, device_id=last_to_over, device_id_type=MESH)
-    pl.semaphore_signal(barrier, inc=1, device_id=last_from_over, device_id_type=MESH)
-    for k in (jnp.where(mine, 6 + par, 2 - par), jnp.where(mine, 3 - par, 5 + par)):
-        giver = (at_z(NZ - k) * 4 + (1 - h) * 2 + c, e)
-        pl.semaphore_signal(barrier, inc=1, device_id=giver, device_id_type=MESH)
 
     deep = iota((T, T), 0)
     lane = iota((T, T), 1)
@@ -265,10 +265,10 @@
     def by_parity(even, odd):
         return jnp.where(mine, even, odd), jnp.where(mine, odd, even)
 
-    with_0 = at_z(6 - par)
-    with_1 = at_z(2 + par)
-    pairs_0 = ((with_0 + c) % NZ, (with_0 + 1 - c) % NZ)
-    pairs_1 = ((with_1 + NZ - c) % NZ, (with_1 + NZ - 1 + c) % NZ)
+    with_0 = at_z(6 - par), at_z(3 - par)
+    with_1 = at_z(2 + par), at_z(5 + par)
+    pairs_0 = [jnp.where(c == n, with_0[0], with_0[1]) for n in range(2)]
+    pairs_1 = [jnp.where(c == n, with_1[0], with_1[1]) for n in range(2)]
     keep = jnp.where(par == 0, pairs_0[0], pairs_1[0]), jnp.where(par == 0, pairs_1[1], pairs_0[1])
     hand = jnp.where(par == 0, pairs_1[0], pairs_0[0]), jnp.where(par == 0, pairs_0[1], pairs_1[1])
     targets = (by_parity(at_z(4), at_z(jnp.where(c == 0, up, down))), keep, by_parity(z, last_to))
@@ -439,7 +439,7 @@
     gycs[0] = gc_sum
     gy = remote(gycs.at[0], gycs.at[1], p_s.at[0], p_r.at[0], over)
     gy.start()
-    for k in (4, jnp.where(c == 0, 1 + 2 * par, 7 - 2 * par)):
+    for k in (4, jnp.where(c == 0, up, down)):
         zz = at_z(NZ - k)
         remote(zsend.at[0, 0], zrecv.at[zz], z_s.at[0, 0], z_r.at[zz], zdev(zz)).wait_recv()
         total = total + zrecv[zz].astype(F32)

time: 70.2 us -> 70.3 us (level)
  no operation moved by 1% of the time
where the time goes in v6:
time: 70.3 us; the launch traced here: 70.2 us
  Pallas kernels  69.6 us (99%)
    pallas_call x1, Pallas kernels, local(): pl.pallas_call(kernel, out_shape=(pltpu.VMEM((96, T), BF16), pltpu.VMEM((...  67.3 us
    pallas_call x1, Pallas kernels, settle(): pl.pallas_call(settle_kernel, out_shape=tuple((jax.ShapeDtypeStruct(a.sha...  2.25 us

profile of v6, /device:TPU:1, one launch (start us, length us, event | category | flops | bytes accessed | tf_op | source)
XLA Modules:
  0.0 70.2 jit_solution(10436128306613692643)
XLA Ops:
  0.6 67.3 %moe_layer.1 = (bf16[96,128]{1,0:T(8,128)(2,1)S(1)}, bf16[96,128]{1,0:T(8,128)(2,1)S(1)}, f32[2,128]{1,0:T(2,128)S(1)}, bf16[3072,256]{1,0:T(8,128)(2,1)S(1)}, b...) custom-call(bf16[128,3072]{1,0:T(8,128)(2,1)} %tok_hbm.1, s32[2,128]{1,0:T(2,128)} %bitcast.14, ...), custom_call_target="tpu_custom_call" | custom-call | tf_op jit(solution)/shard_map/moe_layer/pallas_call | solution.py:505
  68.0 2.3 %settle.1 = (bf16[96,128]{1,0:T(8,128)(2,1)}, bf16[96,128]{1,0:T(8,128)(2,1)}, f32[2,128]{1,0:T(2,128)}, bf16[3072,256]{1,0:T(8,128)(2,1)}, bf16[3072,256]{1,0:T(8,128)(2,1)}, /*index=5*/bf16[256,3072]{1,0:T(8,128)(2,1)}) custom-call(bf16[96,128]{1,0:T(8,128)(2,1)S(1)} %get-tuple-element.18.refs_0_, bf16[96,128]{1,0:T(8,128)(2,1)S(1)} %get-tuple-element.19.refs_1_, ...), custom_call_target="tpu_custom_call" | custom-call | tf_op jit(solution)/shard_map/settle/pallas_call | solution.py:490
